TPU v7x, 128 devices: a whole 4x4x4 slice. The times are simulated.
128 devices in a mesh: mode: 4 (over x), row: 32 (over z, y, core).
Axes of the slice: x: 4, y: 4, z: 4, core: 2. Of those that a mesh axis runs over, the one named last changes fastest.
Arguments:
- initial_modes: float32 [4, 2, 2048, 2048], P('mode', None, 'row'), may hold values from -8 to 8
- mirror_phase: float32 [2048, 2048], P('row'), may hold values from -3.1416 to 3.1416, as said below
- aperture: int32 [2048, 2048], P('row'), may hold values from 0 to 1, as said below
Outputs:
- modes: float32 [4, 2, 2048, 2048], P('mode', None, 'row')
- rayleigh: float32 [2, 2, 4, 4], replicated
Inputs may be any that keep to these rules, and one draw needn't show every extreme that they name: `mirror_phase`: the mirror's curvature plus its aberrations, wrapped to one turn. `aperture`: 1 where the mirror reflects, 0 where light leaves the resonator.
All inputs are finite; a program needn't handle non-finite values.
Results may differ from a plain program's by a relative error of at most 0.00028.
Values sent between devices are 32-bit elements; how exact they have to be, the bound alone decides.
A program may use at most 128 MiB of HBM per device.

v0:
```python
import math

import jax
import jax.numpy as jnp
from jax import lax
from jax.sharding import PartitionSpec as P

ITERS = 3


def complex_einsum(formula, left_real, left_imag, right_real, right_imag):

    def product(first_arg, second_arg):
        return jnp.einsum(formula, first_arg, second_arg, precision=lax.Precision.HIGHEST)

    real_part = product(left_real, right_real) - product(left_imag, right_imag)
    imag_part = product(left_real, right_imag) + product(left_imag, right_real)
    return (real_part, imag_part)


def complex_times(left_real, left_imag, right_real, right_imag):
    return (
        left_real * right_real - left_imag * right_imag,
        left_real * right_imag + left_imag * right_real,
    )


def dft_parts(length, direction):
    counter = jnp.arange(length, dtype=jnp.int32)
    phase = counter[:, None] * counter[None, :] % length
    angle = direction * 2.0 * math.pi / length * phase.astype(jnp.float32)
    return (jnp.cos(angle), jnp.sin(angle))


def block_matrix(cos_part, sin_part):
    upper = jnp.stack([cos_part, sin_part], axis=1)
    lower = jnp.stack([-sin_part, cos_part], axis=1)
    return jnp.stack([upper, lower], axis=0)


def twiddle_parts(outer_len, inner_len, total, direction):
    phase = (
        jnp.arange(outer_len, dtype=jnp.int32)[:, None]
        * jnp.arange(inner_len, dtype=jnp.int32)[None, :]
        % total
    )
    angle = direction * 2.0 * math.pi / total * phase.astype(jnp.float32)
    return (jnp.cos(angle), jnp.sin(angle))


def transfer_grid(outer_len, inner_len):
    total = outer_len * inner_len
    wave = (
        jnp.arange(outer_len, dtype=jnp.int32)[:, None]
        + outer_len * jnp.arange(inner_len, dtype=jnp.int32)[None, :]
    )
    signed = jnp.where(wave < total // 2, wave, wave - total)
    square = signed * signed % (2 * total)
    angle = -math.pi / total * square.astype(jnp.float32)
    return (jnp.cos(angle), jnp.sin(angle))


def rotate_planes(parts, cos_part, sin_part):
    real_part = parts[:, 0]
    imag_part = parts[:, 1]
    return jnp.stack(
        [real_part * cos_part - imag_part * sin_part, real_part * sin_part + imag_part * cos_part],
        axis=1,
    )


def section(formula, parts, matrix):
    return jnp.einsum(formula, parts, matrix, precision=lax.Precision.HIGHEST)


def line_propagate(fields):
    length = fields.shape[-1]
    inner_len = min(length, 128)
    outer_len = length // inner_len
    parts = fields.reshape(fields.shape[:-1] + (outer_len, inner_len))
    fwd_outer = block_matrix(*dft_parts(outer_len, -1.0))
    fwd_inner = block_matrix(*dft_parts(inner_len, -1.0))
    back_outer = block_matrix(*dft_parts(outer_len, 1.0))
    back_inner = block_matrix(*dft_parts(inner_len, 1.0))
    twist_cos, twist_sin = twiddle_parts(outer_len, inner_len, length, -1.0)
    gain_cos, gain_sin = transfer_grid(outer_len, inner_len)
    parts = section("mprba,pbqc->mqrca", parts, fwd_outer)
    parts = rotate_planes(parts, twist_cos, twist_sin)
    parts = section("mprca,paqd->mqrcd", parts, fwd_inner)
    parts = rotate_planes(parts, gain_cos, gain_sin)
    parts = section("mprcd,pdqa->mqrca", parts, back_inner)
    parts = rotate_planes(parts, twist_cos, -twist_sin)
    parts = section("mprca,pcqb->mqrba", parts, back_outer)
    return (parts * (1.0 / length)).reshape(fields.shape)


def turn_propagate(fields):
    return line_propagate(
        lax.all_to_all(jnp.swapaxes(fields, 2, 3), "row", split_axis=2, concat_axis=3, tiled=True)
    )


def turn(fields):
    return lax.all_to_all(
        jnp.swapaxes(fields, 2, 3), "row", split_axis=2, concat_axis=3, tiled=True
    )


def spread(fields):
    return lax.all_to_all(fields, "mode", split_axis=3, concat_axis=0, tiled=True)


def unspread(fields):
    return lax.all_to_all(fields, "mode", split_axis=0, concat_axis=3, tiled=True)


def apply_mirror(fields, planes):
    real_part, imag_part = complex_times(fields[:, 0], fields[:, 1], planes[0], planes[1])
    return jnp.stack([real_part, imag_part], axis=1)


def inner_parts(left, right):
    count = left.shape[0]
    left_real = left[:, 0].reshape(count, -1)
    left_imag = left[:, 1].reshape(count, -1)
    right_real = right[:, 0].reshape(count, -1)
    right_imag = right[:, 1].reshape(count, -1)

    def contract(first_arg, second_arg):
        return lax.dot_general(
            first_arg, second_arg, (((1,), (1,)), ((), ())), precision=lax.Precision.HIGHEST
        )

    real_part = contract(left_real, right_real) + contract(left_imag, right_imag)
    imag_part = contract(left_real, right_imag) - contract(left_imag, right_real)
    return (real_part, imag_part)


def reduce_gram(images, earlier):
    gram_real, gram_imag = inner_parts(images, images)
    if earlier is None:
        proj_real = jnp.zeros_like(gram_real)
        proj_imag = jnp.zeros_like(gram_imag)
    else:
        proj_real, proj_imag = inner_parts(earlier, images)
    return lax.psum((gram_real, gram_imag, proj_real, proj_imag), ("mode", "row"))


def cholesky_parts(gram_real, gram_imag):
    size = gram_real.shape[0]
    counter = jnp.arange(size)
    cols_real = []
    cols_imag = []
    for column in range(size):
        vec_real = gram_real[:, column]
        vec_imag = gram_imag[:, column]
        for earlier in range(column):
            part_real = cols_real[earlier]
            part_imag = cols_imag[earlier]
            conj_real = part_real[column]
            conj_imag = part_imag[column]
            vec_real = vec_real - (part_real * conj_real + part_imag * conj_imag)
            vec_imag = vec_imag - (part_imag * conj_real - part_real * conj_imag)
        pivot = jnp.sqrt(vec_real[column])
        cols_real.append(jnp.where(counter >= column, vec_real / pivot, 0.0))
        cols_imag.append(jnp.where(counter > column, vec_imag / pivot, 0.0))
    return (jnp.stack(cols_real, axis=1), jnp.stack(cols_imag, axis=1))


def inverse_adjoint(lower_real, lower_imag):
    size = lower_real.shape[0]
    identity = jnp.eye(size, dtype=lower_real.dtype)
    rows_real = []
    rows_imag = []
    for target in range(size):
        acc_real = identity[target]
        acc_imag = jnp.zeros((size,), lower_real.dtype)
        for earlier in range(target):
            coef_real = lower_real[target, earlier]
            coef_imag = lower_imag[target, earlier]
            acc_real = acc_real - (coef_real * rows_real[earlier] - coef_imag * rows_imag[earlier])
            acc_imag = acc_imag - (coef_real * rows_imag[earlier] + coef_imag * rows_real[earlier])
        diag_value = lower_real[target, target]
        rows_real.append(acc_real / diag_value)
        rows_imag.append(acc_imag / diag_value)
    solved_real = jnp.stack(rows_real, axis=0)
    solved_imag = jnp.stack(rows_imag, axis=0)
    return (solved_real.T, -solved_imag.T)


def rotate(fields, mix_real, mix_imag):
    real_part, imag_part = complex_einsum(
        "irc,ij->jrc", fields[:, 0], fields[:, 1], mix_real, mix_imag
    )
    return jnp.stack([real_part, imag_part], axis=1)


def body(initial_modes, mirror_phase, aperture):
    grid_side = initial_modes.shape[3]
    opening = aperture.astype(jnp.float32)
    planes = jnp.stack([opening * jnp.cos(mirror_phase), opening * jnp.sin(mirror_phase)])
    rayleigh_list = []
    basis_now = initial_modes
    earlier = None
    for iteration in range(ITERS):
        fields = basis_now
        fields = turn(turn_propagate(line_propagate(fields)))
        fields = apply_mirror(fields, planes)
        fields = turn_propagate(line_propagate(fields))
        images = spread(turn(fields))
        gram_real, gram_imag, proj_real, proj_imag = reduce_gram(images, earlier)
        if iteration > 0:
            rayleigh_list.append(jnp.stack([proj_real, proj_imag]))
        lower_real, lower_imag = cholesky_parts(gram_real, gram_imag)
        inv_real, inv_imag = inverse_adjoint(lower_real, lower_imag)
        earlier = rotate(images, inv_real, inv_imag)
        basis_now = unspread(earlier)
    return (basis_now * grid_side, jnp.stack(rayleigh_list) * grid_side)


def solution(mesh):
    in_specs = (P("mode", None, "row", None), P("row", None), P("row", None))
    out_specs = (P("mode", None, "row", None), P())
    return jax.shard_map(body, mesh=mesh, in_specs=in_specs, out_specs=out_specs, check_vma=False)
```

profile of v0, /device:TPU:1, one launch (start us, length us, event | category | flops | bytes accessed | tf_op | source)
XLA Modules:
  0.0 1072.4 jit_solution(6034991820233747125)
XLA Ops:
  15.2 27.0 %all_to_all.291 = f32[32,1,8192]{2,1,0:T(1,128)S(1)} all-to-all(f32[32,1,8192]{2,1,0:T(1,128)} %reshape.1647), channel_id=1, replica_groups=mesh['mode'=4,'row'=32] {'row'}, dimensions={0} | all-to-all | bytes 2097152 | tf_op jit(solution)/shard_map/all_to_all | solution.py:99
  66.2 21.3 %all_to_all.292 = f32[32,1,8192]{2,1,0:T(1,128)S(1)} all-to-all(f32[32,1,8192]{2,1,0:T(1,128)} %reshape.1649), channel_id=1, replica_groups=mesh['mode'=4,'row'=32] {'row'}, dimensions={0} | all-to-all | bytes 2097152 | tf_op jit(solution)/shard_map/all_to_all | solution.py:104
  87.5 4.4 reduce.67
  115.3 21.5 %all_to_all.293 = f32[32,1,8192]{2,1,0:T(1,128)S(1)} all-to-all(f32[32,1,8192]{2,1,0:T(1,128)} %reshape.1651), channel_id=1, replica_groups=mesh['mode'=4,'row'=32] {'row'}, dimensions={0} | all-to-all | bytes 2097152 | tf_op jit(solution)/shard_map/all_to_all | solution.py:99
  160.3 21.3 %all_to_all.294 = f32[32,1,8192]{2,1,0:T(1,128)S(1)} all-to-all(f32[32,1,8192]{2,1,0:T(1,128)} %reshape.1653), channel_id=1, replica_groups=mesh['mode'=4,'row'=32] {'row'}, dimensions={0} | all-to-all | bytes 2097152 | tf_op jit(solution)/shard_map/all_to_all | solution.py:104
  196.2 18.2 %all_to_all.295 = f32[4,1,65536]{2,1,0:T(1,128)S(1)} all-to-all(f32[4,1,65536]{2,1,0:T(1,128)S(1)} %reshape.1655), channel_id=1, replica_groups=mesh['mode'=4,'row'=32] {'mode'}, dimensions={0} | all-to-all | bytes 2097152 | tf_op jit(solution)/shard_map/all_to_all | solution.py:110
  233.7 64.4 %all-reduce.2 = (f32[4,4]{1,0:T(4,128)S(1)}, f32[4,4]{1,0:T(4,128)S(1)}) all-reduce(f32[4,4]{1,0:T(4,128)S(1)} %fusion.30, f32[4,4]{1,0:T(4,128)S(1)} %fusion.31), channel_id=1, replica_groups=mesh['mode'=4,'row'=32] {'mode','row'}, use_global_device_ids=true, to_apply=%region_0.1 | all-reduce | flops 32 | bytes 256 | tf_op jit(solution)/shard_map/psum | solution.py:146
  324.1 9.3 subtract_divide_fusion.13
  342.1 16.9 %all_to_all.296 = f32[4,2,64,512]{3,2,1,0:T(8,128)S(1)} all-to-all(f32[4,2,64,512]{3,2,1,0:T(8,128)S(1)} %copy.326), channel_id=1, replica_groups=mesh['mode'=4,'row'=32] {'mode'}, dimensions={0} | all-to-all | bytes 2097152 | tf_op jit(solution)/shard_map/all_to_all | solution.py:114
  371.6 23.3 %all_to_all.297 = f32[32,1,8192]{2,1,0:T(1,128)S(1)} all-to-all(f32[32,1,8192]{2,1,0:T(1,128)} %reshape.1657), channel_id=1, replica_groups=mesh['mode'=4,'row'=32] {'row'}, dimensions={0} | all-to-all | bytes 2097152 | tf_op jit(solution)/shard_map/all_to_all | solution.py:99
  418.3 21.3 %all_to_all.298 = f32[32,1,8192]{2,1,0:T(1,128)S(1)} all-to-all(f32[32,1,8192]{2,1,0:T(1,128)} %reshape.1659), channel_id=1, replica_groups=mesh['mode'=4,'row'=32] {'row'}, dimensions={0} | all-to-all | bytes 2097152 | tf_op jit(solution)/shard_map/all_to_all | solution.py:104
  463.7 21.4 %all_to_all.299 = f32[32,1,8192]{2,1,0:T(1,128)S(1)} all-to-all(f32[32,1,8192]{2,1,0:T(1,128)} %reshape.1661), channel_id=1, replica_groups=mesh['mode'=4,'row'=32] {'row'}, dimensions={0} | all-to-all | bytes 2097152 | tf_op jit(solution)/shard_map/all_to_all | solution.py:99
  508.5 21.3 %all_to_all.300 = f32[32,1,8192]{2,1,0:T(1,128)S(1)} all-to-all(f32[32,1,8192]{2,1,0:T(1,128)} %reshape.1663), channel_id=1, replica_groups=mesh['mode'=4,'row'=32] {'row'}, dimensions={0} | all-to-all | bytes 2097152 | tf_op jit(solution)/shard_map/all_to_all | solution.py:104
  544.3 17.6 %all_to_all.301 = f32[4,1,65536]{2,1,0:T(1,128)S(1)} all-to-all(f32[4,1,65536]{2,1,0:T(1,128)S(1)} %reshape.1665), channel_id=1, replica_groups=mesh['mode'=4,'row'=32] {'mode'}, dimensions={0} | all-to-all | bytes 2097152 | tf_op jit(solution)/shard_map/all_to_all | solution.py:110
  581.3 63.4 %all-reduce.1 = (f32[4,4]{1,0:T(4,128)S(1)}, f32[4,4]{1,0:T(4,128)S(1)}) all-reduce(f32[4,4]{1,0:T(4,128)S(1)} %fusion.32, f32[4,4]{1,0:T(4,128)S(1)} %fusion.33), channel_id=1, replica_groups=mesh['mode'=4,'row'=32] {'mode','row'}, use_global_device_ids=true, to_apply=%region_2.3 | all-reduce | flops 32 | bytes 256 | tf_op jit(solution)/shard_map/psum | solution.py:146
  670.4 9.3 subtract_divide_fusion.7
  688.4 16.9 %all_to_all.302 = f32[4,2,64,512]{3,2,1,0:T(8,128)S(1)} all-to-all(f32[4,2,64,512]{3,2,1,0:T(8,128)S(1)} %copy.361), channel_id=1, replica_groups=mesh['mode'=4,'row'=32] {'mode'}, dimensions={0} | all-to-all | bytes 2097152 | tf_op jit(solution)/shard_map/all_to_all | solution.py:114
  719.3 23.4 %all_to_all.303 = f32[32,1,8192]{2,1,0:T(1,128)} all-to-all(f32[32,1,8192]{2,1,0:T(1,128)S(1)} %reshape.1667), channel_id=1, replica_groups=mesh['mode'=4,'row'=32] {'row'}, dimensions={0} | all-to-all | bytes 2097152 | tf_op jit(solution)/shard_map/all_to_all | solution.py:99
  742.7 4.4 reduce.76
  766.7 21.2 %all_to_all.304 = f32[32,1,8192]{2,1,0:T(1,128)} all-to-all(f32[32,1,8192]{2,1,0:T(1,128)S(1)} %reshape.1669), channel_id=1, replica_groups=mesh['mode'=4,'row'=32] {'row'}, dimensions={0} | all-to-all | bytes 2097152 | tf_op jit(solution)/shard_map/all_to_all | solution.py:104
  787.9 4.4 reduce.77
  814.7 21.0 %all_to_all.305 = f32[32,1,8192]{2,1,0:T(1,128)} all-to-all(f32[32,1,8192]{2,1,0:T(1,128)S(1)} %reshape.1671), channel_id=1, replica_groups=mesh['mode'=4,'row'=32] {'row'}, dimensions={0} | all-to-all | bytes 2097152 | tf_op jit(solution)/shard_map/all_to_all | solution.py:99
  835.7 4.4 reduce.78
  856.2 4.6 reshape.1673
  860.8 4.6 all-to-all-start.15
  865.5 17.3 %all-to-all-done.15 = f32[32,1,8192]{2,1,0:T(1,128)} async-done(((f32[32,1,8192]{2,1,0:T(1,128)}), f32[32,1,8192]{2,1,0:T(1,128)}, u32[]{:S(2)}, u32[]{:S(2)}) %all-to-all-start.15) | async-done | bytes 1048608 | tf_op jit(solution)/shard_map/all_to_all | solution.py:104
  882.8 5.4 reduce.79
  894.6 4.7 reshape.1675
  913.2 4.7 all-to-all-done.16
  944.7 63.5 %all-reduce = (f32[4,4]{1,0:T(4,128)S(1)}, f32[4,4]{1,0:T(4,128)S(1)}, f32[1,4,4]{2,1,0:T(4,128)S(1)}, f32[1,4,4]{2,1,0:T(4,128)S(1)}, f32[1,4,4]{2,1,0:T(4,128)S(1)}, /*index=5*/f32[1,4,4]{2,1,0:T(4,128)S(1)}) all-reduce(f32[4,4]{1,0:T(4,128)S(1)} %fusion.34, ...), channel_id=1, replica_groups=mesh['mode'=4,'row'=32] {'mode','row'}, use_global_device_ids=true, to_apply=%region_4.5 | all-reduce | flops 96 | bytes 768 | tf_op jit(solution)/shard_map/psum | solution.py:146
  1034.0 9.4 subtract_divide_fusion.1
  1056.9 13.9 %all-to-all-done.17 = f32[4,2,64,512]{3,2,1,0:T(8,128)S(1)} async-done(((f32[4,2,64,512]{3,2,1,0:T(8,128)}), f32[4,2,64,512]{3,2,1,0:T(8,128)S(1)}, u32[]{:S(2)}, u32[]{:S(2)}) %all-to-all-start.17) | async-done | bytes 1048608 | tf_op jit(solution)/shard_map/all_to_all | solution.py:114
  (359 shorter events, 442.6 us)
Async XLA Ops:
  103.0 0.8 copy-start
  340.3 1.6 copy-start.3
  341.3 0.8 copy-start.5
  449.3 2.6 copy-start.1
  686.6 1.6 copy-start.7
  687.6 0.8 copy-start.9
  799.3 2.9 copy-start.2
  860.8 22.0 %all-to-all-start.15 = ((f32[32,1,8192]{2,1,0:T(1,128)}), f32[32,1,8192]{2,1,0:T(1,128)}, u32[]{:S(2)}, u32[]{:S(2)}) async-start(f32[32,1,8192]{2,1,0:T(1,128)} %reshape.1673), calls=%async_computation.15 | async-start | bytes 2097152 | tf_op jit(solution)/shard_map/all_to_all | solution.py:104
  894.6 8.5 copy-start.4
  899.3 6.3 copy-start.6
  899.3 18.6 %all-to-all-start.16 = ((f32[4,1,65536]{2,1,0:T(1,128)}), f32[4,1,65536]{2,1,0:T(1,128)S(1)}, u32[]{:S(2)}, u32[]{:S(2)}) async-start(f32[4,1,65536]{2,1,0:T(1,128)} %reshape.1675), calls=%async_computation.16 | async-start | bytes 2097152 | tf_op jit(solution)/shard_map/all_to_all | solution.py:110
  929.3 5.0 copy-start.8
  929.4 10.0 copy-start.10
  1052.8 18.0 %all-to-all-start.17 = ((f32[4,2,64,512]{3,2,1,0:T(8,128)}), f32[4,2,64,512]{3,2,1,0:T(8,128)S(1)}, u32[]{:S(2)}, u32[]{:S(2)}) async-start(f32[4,2,64,512]{3,2,1,0:T(8,128)} %copy.396), calls=%async_computation.17 | async-start | bytes 2097152 | tf_op jit(solution)/shard_map/all_to_all | solution.py:114
where the time goes:
time: 1080 us; the launch traced here: 1070 us
  blocking collectives  505 us (47%)
  local copies, waits for them, and re-layouts  212 us (20%)
  other arithmetic  155 us (14%)
  matrix products  129 us (12%)
  waiting for transfers between devices  35.8 us (3%)
  between operations  24.2 us (2%)
  starting transfers between devices  12 us (1%)
    psum x3, blocking collectives, reduce_gram(): lax.psum((gram_real, gram_imag, proj_real, proj_imag), ('mode', 'row'))  191 us
    all_to_all x6, blocking collectives, turn_propagate(): lax.all_to_all(jnp.swapaxes(fields, 2, 3), 'row', split_axis=2, concat_ax...  138 us
    all_to_all x5, blocking collectives, turn(): lax.all_to_all(jnp.swapaxes(fields, 2, 3), 'row', split_axis=2, concat_ax...  106 us
    unnamed x59, local copies, waits for them, and re-layouts  96.9 us
    dot_general x48, matrix products, section(): return jnp.einsum(formula, parts, matrix, precision=lax.Precision.HIGHEST)  67 us
    dot_general x20, matrix products, contract(): lax.dot_general(first_arg, second_arg, (((1,), (1,)), ((), ())), precisio...  49.8 us
    all_to_all x2, blocking collectives, spread(): lax.all_to_all(fields, 'mode', split_axis=3, concat_axis=0, tiled=True)  35.8 us
    all_to_all x2, blocking collectives, unspread(): lax.all_to_all(fields, 'mode', split_axis=0, concat_axis=3, tiled=True)  33.7 us
  transfers between devices with their start and end apart: 3, of which 3 were waited for; matrix products, arithmetic and copies ran while one was open for 1% of the time, Pallas kernels for 0%

commit v1 on v0

v1 whole, which is shorter than its diff:
```python
import functools

import jax
import jax.numpy as jnp
import numpy as np
from jax import lax
from jax.experimental import pallas as pl
from jax.experimental.pallas import tpu as pltpu
from jax.sharding import PartitionSpec as P


SIDE = 2048
F32 = jnp.float32
BF16 = jnp.bfloat16
LANES = 128


def chirp(index, length):
    square = (index.astype(np.int64) ** 2) % (2 * length)
    return np.exp(1j * np.pi * square / length)


def planes_of(table):
    both = np.concatenate([table.real, table.imag], axis=-1)
    return both.astype(np.float32)


def make_tables():
    lane = np.arange(LANES)
    order = 16 * (lane % 8) + lane // 8
    tables = {}
    for outer in (16, 8):
        length = outer * LANES
        gain = np.exp(-0.25j * np.pi) / np.sqrt(length)
        block = np.arange(outer)
        natural = chirp(LANES * block[:, None] + lane[None, :], length)
        strided = chirp(block[:, None] + outer * lane[None, :], length)
        twist = np.exp(-2j * np.pi * (block[:, None] * lane[None, :] % length) / length)
        tables["nat", outer] = planes_of(natural)
        tables["nat_gain", outer] = planes_of(natural * gain)
        tables["str", outer] = planes_of(strided)
        tables["str_gain", outer] = planes_of(strided * gain)
        tables["str_p", outer] = planes_of(strided[:, order])
        tables["str_gain_p", outer] = planes_of((strided * gain)[:, order])
        tables["twist", outer] = planes_of(twist)
    wave = np.exp(-2j * np.pi * (lane[:, None] * lane[None, :] % LANES) / LANES)
    for name, matrix in (("w", wave), ("w_out", wave[:, order]), ("w_in", wave[order, :])):
        upper = np.concatenate([matrix.real, matrix.imag], axis=1)
        lower = np.concatenate([-matrix.imag, matrix.real], axis=1)
        full = np.concatenate([upper, lower], axis=0).astype(np.float32)
        high = full.astype(jnp.bfloat16)
        low = (full - high.astype(np.float32)).astype(jnp.bfloat16)
        tables[name] = np.stack([high, low])
    pick = np.zeros((256, 256), np.float32)
    pick[2 * lane, lane] = 1.0
    pick[2 * lane + 1, LANES + lane] = 1.0
    tables["pick"] = pick.astype(jnp.bfloat16)
    return tables


TABLES = make_tables()


def times(ar, ai, br, bi):
    return ar * br - ai * bi, ar * bi + ai * br


def small_dft(values):
    count = len(values)
    if count == 1:
        return values
    even = small_dft(values[0::2])
    odd = small_dft(values[1::2])
    first, second = [], []
    for index in range(count // 2):
        re, im = odd[index]
        if index == 0:
            tr, ti = re, im
        elif 4 * index == count:
            tr, ti = im, -re
        elif 8 * index == count:
            half = float(np.sqrt(0.5))
            tr, ti = (re + im) * half, (im - re) * half
        elif 8 * index == 3 * count:
            half = float(np.sqrt(0.5))
            tr, ti = (im - re) * half, -(re + im) * half
        else:
            angle = -2.0 * np.pi * index / count
            tr, ti = times(re, im, float(np.cos(angle)), float(np.sin(angle)))
        er, ei = even[index]
        first.append((er + tr, ei + ti))
        second.append((er - tr, ei - ti))
    return first + second


def matmul(values, w_ref):
    high = values.astype(BF16)
    low = (values - high.astype(F32)).astype(BF16)
    w_high = w_ref[0]
    w_low = w_ref[1]

    def dot(left, right):
        return jnp.dot(left, right, preferred_element_type=F32)

    return dot(high, w_high) + dot(low, w_high) + dot(high, w_low)


def split(values):
    return values[..., :LANES], values[..., LANES:]


def swap(first, second, stride):
    lane = lax.broadcasted_iota(jnp.int32, first.shape, first.ndim - 1)
    keep = (lane & stride) == 0
    axis = first.ndim - 1
    return (
        jnp.where(keep, first, pltpu.roll(second, stride, axis)),
        jnp.where(keep, pltpu.roll(first, LANES - stride, axis), second),
    )


def swap_bits(arrays, strides):
    arrays = list(arrays)
    for bit, stride in enumerate(strides):
        for low in range(len(arrays)):
            if not low >> bit & 1:
                high = low | 1 << bit
                arrays[low], arrays[high] = swap(arrays[low], arrays[high], stride)
    return arrays


def put(ref, block, rows, re, im):
    ref[block, rows, :LANES] = re
    ref[block, rows, LANES:] = im


def outer_dft(src, dst, outer, pre, post, index_in, index_out):
    def tile(step, carry):
        rows = pl.ds(pl.multiple_of(step * 8, 8), 8)
        for group in range(16 // outer):
            values = []
            for n in range(outer):
                at = index_in(group, n)
                re, im = src[at, rows, :LANES], src[at, rows, LANES:]
                if pre is not None:
                    re, im = times(re, im, pre[n : n + 1, :LANES], pre[n : n + 1, LANES:])
                values.append((re, im))
            values = small_dft(values)
            for k in range(outer):
                re, im = values[k]
                if post is not None:
                    re, im = times(re, im, post[k : k + 1, :LANES], post[k : k + 1, LANES:])
                put(dst, index_out(group, k), rows, re, im)
        return carry

    lax.fori_loop(0, 8, tile, 0)


def natural_at(outer):
    return lambda group, n: outer * group + n


def strided_at(outer):
    return lambda group, n: (16 // outer) * n + group


def to_strided(src, tmp, outer, pre, twist, w_ref, sink):
    outer_dft(src, tmp, outer, pre, twist, natural_at(outer), strided_at(outer))
    for part in range(4):
        values = tmp[4 * part : 4 * part + 4].reshape(256, 256)
        result = matmul(values, w_ref).reshape(4, 64, 256)
        for n in range(4):
            sink(4 * part + n, *split(result[n]))


def to_natural(src, tmp, dst, outer, pre, w_ref, twist, post):
    groups = 16 // outer
    for part in range(4):
        pieces = []
        for n in range(4 * part, 4 * part + 4):
            re, im = split(src[n])
            if pre is not None:
                at = n // groups
                re, im = times(re, im, pre[at : at + 1, :LANES], pre[at : at + 1, LANES:])
            pieces.append(jnp.concatenate([re, im], axis=1))
        values = jnp.concatenate(pieces, axis=0)
        tmp[4 * part : 4 * part + 4] = matmul(values, w_ref).reshape(4, 64, 256)
    outer_dft(tmp, dst, outer, twist, post, strided_at(outer), natural_at(outer))


def turned(re, im):
    return jnp.concatenate([re, im], axis=0).T


def send_columns(out, block, tile):
    for x in range(4):
        for b in range(2):
            out[32 * x + 2 * block + b] = tile[32 * x + 16 * b : 32 * x + 16 * b + 16]


def row_source(parity, block, group):
    return 32 * (2 * (group & 1) + parity) + 4 * block + (group >> 1)


def column_source(block, group):
    return 32 * (group >> 1) + 2 * block + (group & 1)


def first_kernel(modes, nat, twist, post, w, out, src, tmp):
    for n in range(16):
        lanes = slice(LANES * n, LANES * n + LANES)
        put(src, n, slice(None), modes[0, 0, :, lanes], modes[0, 1, :, lanes])

    def sink(block, re, im):
        re, im = times(re, im, *split(post[block : block + 1]))
        send_columns(out, block, turned(re, im))

    to_strided(src, tmp, 16, nat, twist, w, sink)


def mirror_kernel(phase, aperture, pick, out, rows_out, tile, lines):
    x = lax.axis_index("mode")
    for part in range(4):
        lanes = pl.ds(pl.multiple_of(512 * x + LANES * part, LANES), LANES)
        angle = phase[:, lanes]
        opening = aperture[:, lanes].astype(F32)
        parts = []
        for plane in (opening * jnp.cos(angle), opening * jnp.sin(angle)):
            tiles = plane.reshape(4, 2, 8, LANES)
            for half in range(2):
                for step in range(4):
                    parts.append(tiles[step, half])
        tile[LANES * part : LANES * part + LANES] = jnp.concatenate(parts, axis=0).T
    for block in range(16):
        for b in range(2):
            out[2 * block + b] = tile[pl.ds(256 * b + block, 16, stride=16), :]
    base = 32 * (x // 2) + lax.rem(x, 2)
    for n in range(16):
        lanes = slice(LANES * n, LANES * n + LANES)
        lines[0, 64 * n : 64 * n + 64] = phase[:, lanes]
        lines[1, 64 * n : 64 * n + 64] = aperture[:, lanes].astype(F32)
    for k in range(8):
        starts = [pl.ds(64 * n + base, 16, stride=2) for n in (2 * k, 2 * k + 1)]
        angle = jnp.concatenate([lines.at[0][at, :] for at in starts], axis=1)
        opening = jnp.concatenate([lines.at[1][at, :] for at in starts], axis=1)
        for plane, part in enumerate((opening * jnp.cos(angle), opening * jnp.sin(angle))):
            high = part.astype(BF16)
            rest = part - high.astype(F32)
            middle = rest.astype(BF16)
            low = (rest - middle.astype(F32)).astype(BF16)
            total = sum(
                jnp.dot(piece, pick[...], preferred_element_type=F32)
                for piece in (low, middle, high)
            )
            lanes = slice(LANES * plane, LANES * plane + LANES)
            rows_out[k, :, lanes] = total[:, :LANES]
            rows_out[8 + k, :, lanes] = total[:, LANES:]


def mirror_columns(got, out):
    arrays = {}
    for top in range(8):
        for b in range(2):
            low, high = swap(got[4 * top + b], got[4 * top + 2 + b], 64)
            arrays[top, b, 0], arrays[top, b, 1] = low, high
    for plane in range(2):
        done = swap_bits(
            [arrays[index % 8, index // 8, plane] for index in range(16)], (1, 2, 4, 32)
        )
        for block in range(16):
            out[block, :, LANES * plane : LANES * plane + LANES] = done[block]


def by_mode(values):
    return values.reshape(4, 16, LANES)


def cell_times(re, im, er, ei):
    re, im = times(by_mode(re), by_mode(im), er[None], ei[None])
    return re.reshape(64, LANES), im.reshape(64, LANES)


def second_kernel(
    got, mirror, nat, twist, post, w_out, pre8, twist8, post8, w_in, out, cells, mirror_out, src, tmp
):
    mirror_columns(mirror, mirror_out)
    for mode in range(4):
        for n in range(16):
            re, im = swap(got[32 * mode + 2 * n], got[32 * mode + 2 * n + 1], 64)
            put(src, n, slice(16 * mode, 16 * mode + 16), re, im)

    def sink(block, re, im):
        er, ei = split(mirror_out[block])
        er, ei = times(er, ei, *split(post[block : block + 1]))
        put(cells, block, slice(None), *cell_times(re, im, er, ei))

    to_strided(src, tmp, 16, nat, twist, w_out, sink)
    to_natural(cells, tmp, src, 8, pre8, w_in, twist8, post8)
    for parity in range(2):
        for block in range(8):
            tile = turned(*split(src[8 * parity + block]))
            for group in range(8):
                out[row_source(parity, block, group)] = tile[16 * group : 16 * group + 16]


def third_kernel(
    got, mirror, pre8, w, twist8, post8, nat8, str8, out, out_cells, src, tmp, tile
):
    for block in range(16):
        done = swap_bits([got[column_source(block, group)] for group in range(8)], (16, 32, 64))
        for mode in range(4):
            put(src, block, slice(16 * mode, 16 * mode + 16), done[mode], done[4 + mode])
    to_natural(src, tmp, src, 8, pre8, w, twist8, post8)
    for block in range(16):
        re, im = cell_times(*split(src[block]), *split(mirror[block]))
        put(src, block, slice(None), re, im)
        tile[...] = turned(re, im)
        parity, k = block // 8, block % 8
        for v in range(8):
            out_cells[column_source(2 * v + parity, k)] = tile[pl.ds(v, 16, stride=8), :]

    def sink(block, re, im):
        at = block // 2
        re, im = times(re, im, *split(str8[at : at + 1]))
        send_columns(out, block, turned(re, im))

    to_strided(src, tmp, 8, nat8, twist8, w, sink)


PAIRS = [(i, j) for i in range(4) for j in range(i, 4)]


def gram(left, right, same):
    pairs = PAIRS if same else [(i, j) for i in range(4) for j in range(4)]

    def step(index, carry):
        block, half = index // 2, lax.rem(index, 2)
        a, b = [], []
        for mode in range(4):
            rows = pl.ds(pl.multiple_of(16 * mode + 8 * half, 8), 8)
            a.append((left[block, rows, :LANES], left[block, rows, LANES:]))
            b.append(a[-1] if same else (right[block, rows, :LANES], right[block, rows, LANES:]))
        result = []
        at = 0
        for i, j in pairs:
            (ar, ai), (br, bi) = a[i], b[j]
            result.append(carry[at] + (ar * br + ai * bi))
            at += 1
            if not (same and i == j):
                result.append(carry[at] + (ar * bi - ai * br))
                at += 1
        return tuple(result)

    count = 16 if same else 32
    zero = tuple(jnp.zeros((8, LANES), F32) for _ in range(count))
    sums = lax.fori_loop(0, 32, step, zero)
    return [jnp.sum(value, axis=0, keepdims=True) for value in sums]


def fourth_kernel(
    got, got_cells, cells, mirror, nat8, twist8, w_out, post8, out, sums, src, tmp, middle
):
    for parity in range(2):
        for block in range(8):
            sources = [row_source(parity, block, group) for group in range(8)]
            done = swap_bits([got[at] for at in sources], (16, 32, 64))
            for mode in range(4):
                rows = slice(16 * mode, 16 * mode + 16)
                put(src, 8 * parity + block, rows, done[mode], done[4 + mode])
            done = swap_bits([got_cells[at] for at in sources], (16, 32, 64))
            for mode in range(4):
                rows = slice(16 * mode, 16 * mode + 16)
                put(tmp, 8 * parity + block, rows, done[mode], done[4 + mode])
    for parity in range(2):
        for mode in range(4):
            rows = slice(16 * mode, 16 * mode + 16)
            for plane in range(2):
                lanes = slice(LANES * plane, LANES * plane + LANES)
                done = swap_bits([tmp[8 * parity + k, rows, lanes] for k in range(8)], (1, 2, 4))
                for k in range(8):
                    middle[2 * k + parity, rows, lanes] = done[k]

    def sink(block, re, im):
        er, ei = split(mirror[block])
        at = block // 2
        er, ei = times(er, ei, *split(post8[at : at + 1]))
        put(out, block, slice(None), *cell_times(re, im, er, ei))

    to_strided(src, tmp, 8, nat8, twist8, w_out, sink)
    rows = gram(cells, cells, True) + gram(middle, middle, True) + gram(out, out, True)
    rows += gram(cells, middle, False) + gram(middle, out, False)
    rows.append(jnp.zeros((16, LANES), F32))
    total = jnp.sum(jnp.concatenate(rows, axis=0).T, axis=0, keepdims=True)
    sums[...] = jnp.broadcast_to(total, (8, LANES))


def unpack_gram(values, start):
    table = {}
    at = start
    for i, j in PAIRS:
        if i == j:
            table[i, j] = (values(at), None)
            at += 1
        else:
            re, im = values(at), values(at + 1)
            table[i, j] = (re, im)
            table[j, i] = (re, -im)
            at += 2
    return table


def inverse_factor(table):
    lower = {}
    for j in range(4):
        for i in range(j, 4):
            re, im = table[i, j]
            for k in range(j):
                ar, ai = lower[i, k]
                br, bi = lower[j, k]
                re = re - (ar * br + ai * bi)
                if i != j:
                    im = im - (ai * br - ar * bi)
            if i == j:
                pivot = jnp.sqrt(re)
                lower[j, j] = (pivot, jnp.zeros_like(pivot))
                scale = 1.0 / pivot
            else:
                lower[i, j] = (re * scale, im * scale)
    inverse = {}
    for i in range(4):
        scale = 1.0 / lower[i, i][0]
        inverse[i, i] = (scale, jnp.zeros_like(scale))
        for j in range(i):
            re = im = None
            for k in range(j, i):
                pr, pi = times(*lower[i, k], *inverse[k, j])
                re = pr if re is None else re + pr
                im = pi if im is None else im + pi
            inverse[i, j] = (-re * scale, -im * scale)
    return {(j, i): (re, -im) for (i, j), (re, im) in inverse.items()}


def projected(factor, values, start):
    table = {}
    for i in range(4):
        for j in range(4):
            at = start + 2 * (4 * i + j)
            table[i, j] = (values(at), values(at + 1))
    half = {}
    for i in range(4):
        for j in range(4):
            re = im = 0.0
            for k in range(j + 1):
                pr, pi = times(*table[i, k], *factor[k, j])
                re, im = re + pr, im + pi
            half[i, j] = (re, im)
    result = {}
    for i in range(4):
        for j in range(4):
            re = im = 0.0
            for k in range(i + 1):
                fr, fi = factor[k, i]
                pr, pi = times(fr, -fi, *half[k, j])
                re, im = re + pr, im + pi
            result[i, j] = (re, im)
    return result


def fifth_kernel(cells, sums, str_p, w_in, twist, post, out, ray, src, tmp):
    total = jnp.sum(sums[...], axis=0)

    def values(at):
        return jnp.broadcast_to(total[:, at : at + 1], (8, LANES))

    for step in range(2):
        factor = inverse_factor(unpack_gram(values, 16 * step))
        result = projected(factor, values, 48 + 32 * step)
        for i in range(4):
            for j in range(4):
                for plane in range(2):
                    at = 32 * step + 16 * plane + 4 * i + j
                    ray[at : at + 1, :] = result[i, j][plane][0:1] * float(SIDE)
    factor = inverse_factor(unpack_gram(values, 32))
    factor = {key: (re * float(SIDE), im * float(SIDE)) for key, (re, im) in factor.items()}
    to_natural(cells, tmp, src, 16, str_p, w_in, twist, post)
    for block in range(16):
        for half in range(2):
            base = 8 * half
            fields = [
                split(src[block, 16 * mode + base : 16 * mode + base + 8]) for mode in range(4)
            ]
            for j in range(4):
                re = im = 0.0
                for i in range(j + 1):
                    pr, pi = times(*fields[i], *factor[i, j])
                    re, im = re + pr, im + pi
                rows = slice(16 * j + base, 16 * j + base + 8)
                put(tmp, block, rows, re, im)
        pieces = []
        for mode in range(4):
            rows = slice(16 * mode, 16 * mode + 16)
            pieces += [tmp[block, rows, :LANES], tmp[block, rows, LANES:]]
        tile = jnp.concatenate(pieces, axis=0).T
        for half in range(2):
            parts = [tile[64 * half + 16 * q : 64 * half + 16 * q + 16] for q in range(4)]
            done = swap_bits(parts, (32, 64))
            for mode in range(4):
                out[32 * mode + 2 * block + half] = done[mode]


def last_kernel(got, str16, w, twist, post, out, src, tmp):
    for block in range(16):
        done = swap_bits([got[column_source(block, group)] for group in range(8)], (16, 32, 64))
        for q in range(4):
            put(src, block, slice(16 * q, 16 * q + 16), done[2 * q], done[2 * q + 1])
    to_natural(src, tmp, src, 16, str16, w, twist, post)
    for n in range(16):
        lanes = slice(LANES * n, LANES * n + LANES)
        out[0, 0, :, lanes], out[0, 1, :, lanes] = split(src[n])


FIELD = (16, 64, 256)
PACKETS = (128, 16, LANES)


def run(kernel, name, args, tables, outs, scratch):
    arrays = [jnp.asarray(TABLES[key]) for key in tables]
    whole = pl.BlockSpec(memory_space=pltpu.VMEM)
    return pl.pallas_call(
        kernel,
        name=name,
        in_specs=[whole] * (len(args) + len(arrays)),
        out_specs=[whole] * len(outs),
        out_shape=[jax.ShapeDtypeStruct(shape, F32) for shape in outs],
        scratch_shapes=[pltpu.VMEM(shape, F32) for shape in scratch],
        compiler_params=pltpu.CompilerParams(vmem_limit_bytes=48 * 1024 * 1024),
    )(*args, *arrays)


def exchange(packets):
    return lax.all_to_all(packets, ("mode", "row"), split_axis=0, concat_axis=0, tiled=True)


def body(initial_modes, mirror_phase, aperture):
    mirror_send, mirror_rows = run(
        mirror_kernel, "mirror", (mirror_phase, aperture), ["pick"],
        [(32, 16, LANES), (16, 16, 256)], [(512, LANES), (2, 1024, LANES)],
    )
    mirror_got = lax.all_to_all(mirror_send, "row", split_axis=0, concat_axis=0, tiled=True)
    (packets,) = run(
        first_kernel, "first", (initial_modes,),
        [("nat", 16), ("twist", 16), ("str_gain", 16), "w"], [PACKETS], [FIELD, FIELD],
    )
    got = exchange(packets)
    packets, cells_one, mirror_columns_now = run(
        second_kernel, "second", (got, mirror_got),
        [("nat", 16), ("twist", 16), ("str_gain_p", 16), "w_out",
         ("str_p", 8), ("twist", 8), ("nat_gain", 8), "w_in"],
        [PACKETS, FIELD, (16, 16, 256)], [FIELD, FIELD],
    )
    got = exchange(packets)
    packets, packets_cells = run(
        third_kernel, "third", (got, mirror_rows),
        [("str", 8), "w", ("twist", 8), ("nat_gain", 8), ("nat", 8), ("str_gain", 8)],
        [PACKETS, PACKETS], [FIELD, FIELD, (LANES, LANES)],
    )
    got = exchange(packets)
    got_cells = exchange(packets_cells)
    cells_three, sums = run(
        fourth_kernel, "fourth", (got, got_cells, cells_one, mirror_columns_now),
        [("nat", 8), ("twist", 8), "w_out", ("str_gain_p", 8)],
        [FIELD, (8, LANES)], [FIELD, FIELD, FIELD],
    )
    sums = exchange(jnp.broadcast_to(sums[None], (128, 8, LANES)))
    packets, ray = run(
        fifth_kernel, "fifth", (cells_three, sums),
        [("str_p", 16), "w_in", ("twist", 16), ("nat_gain", 16)],
        [PACKETS, (64, LANES)], [FIELD, FIELD],
    )
    got = exchange(packets)
    (modes,) = run(
        last_kernel, "last", (got,),
        [("str", 16), "w", ("twist", 16), ("nat_gain", 16)],
        [(1, 2, 64, SIDE)], [FIELD, FIELD],
    )
    return modes, ray[:, 0].reshape(2, 2, 4, 4)


def solution(mesh):
    in_specs = (P("mode", None, "row", None), P("row", None), P("row", None))
    out_specs = (P("mode", None, "row", None), P())
    return jax.shard_map(body, mesh=mesh, in_specs=in_specs, out_specs=out_specs, check_vma=False)
```

time: 1080 us -> 189 us (0.17)
  blocking collectives: 505 us -> 113 us
  local copies, waits for them, and re-layouts: 212 us -> 3.94 us
  other arithmetic: 155 us -> 0 us
  matrix products: 129 us -> 0 us
  Pallas kernels: 0 us -> 30 us
  between operations: 24.2 us -> 0.86 us
    all_to_all x15 -> x5, blocking collectives: 313 us -> 113 us  [exchange(): lax.all_to_all(packets, ('mode', 'row'), split_axis=0, concat_axis=0, til...]
    psum x3 -> x0, blocking collectives: 191 us -> none  [reduce_gram(): lax.psum((gram_real, gram_imag, proj_real, proj_imag), ('mode', 'row'))]
    dot_general x80 -> x0, matrix products: 129 us -> none  [the longest x48 67 us: section(): return jnp.einsum(formula, parts, matrix, precision=lax.Precision.HIGHEST)]
    unnamed x59 -> x42, local copies, waits for them, and re-layouts: 96.9 us -> 3.08 us
    all_to_all x15 -> x0, other arithmetic: 65.1 us -> none  [the longest x6 27.5 us: turn(): lax.all_to_all(jnp.swapaxes(fields, 2, 3), 'row', split_axis=2, concat_ax...]
    all_to_all x21 -> x0, local copies, waits for them, and re-layouts: 54.7 us -> none  [the longest x9 27.5 us: turn(): lax.all_to_all(jnp.swapaxes(fields, 2, 3), 'row', split_axis=2, concat_ax...]
    div x6 -> x0, other arithmetic: 39.2 us -> none  [the longest x3 27.9 us: inverse_adjoint(): rows_real.append(acc_real / diag_value)]
    pallas_call x0 -> x7, Pallas kernels: none -> 30 us  [run(): pl.pallas_call(kernel, name=name, in_specs=[whole] * (len(args) + len(arr...]
  transfers between devices with their start and end apart: 3 -> 2, of which waited for: 3 -> 2; matrix products, arithmetic and copies ran while one was open for 1% -> 0% of each run, Pallas kernels for 0% -> 1%
where the time goes in v1:
time: 189 us; the launch traced here: 188 us
  blocking collectives  113 us (60%)
  Pallas kernels  30 us (16%)
  waiting for transfers between devices  25.7 us (14%)
  starting transfers between devices  14.5 us (8%)
  local copies, waits for them, and re-layouts  3.94 us (2%)
    all_to_all x5, blocking collectives, exchange(): lax.all_to_all(packets, ('mode', 'row'), split_axis=0, concat_axis=0, til...  113 us
    pallas_call x7, Pallas kernels, run(): pl.pallas_call(kernel, name=name, in_specs=[whole] * (len(args) + len(arr...  30 us
    all_to_all x1, waiting for transfers between devices, exchange(): lax.all_to_all(packets, ('mode', 'row'), split_axis=0, concat_axis=0, til...  18.2 us
    all_to_all x1, starting transfers between devices, body(): lax.all_to_all(mirror_send, 'row', split_axis=0, concat_axis=0, tiled=True)  9.75 us
    all_to_all x1, waiting for transfers between devices, body(): lax.all_to_all(mirror_send, 'row', split_axis=0, concat_axis=0, tiled=True)  7.49 us
    all_to_all x1, starting transfers between devices, exchange(): lax.all_to_all(packets, ('mode', 'row'), split_axis=0, concat_axis=0, til...  4.76 us
  transfers between devices with their start and end apart: 2, of which 2 were waited for; matrix products, arithmetic and copies ran while one was open for 0% of the time, Pallas kernels for 1%

profile of v1, /device:TPU:1, one launch (start us, length us, event | category | flops | bytes accessed | tf_op | source)
XLA Modules:
  0.0 188.3 jit_solution(4776208099547808886)
XLA Ops:
  0.6 1.0 copy-done.4
  1.7 1.0 copy-done.5
  2.7 0.9 copy-done.7
  3.6 2.1 %mirror.1 = (f32[32,16,128]{2,1,0:T(8,128)}, f32[16,16,256]{2,1,0:T(8,128)S(1)}) custom-call(f32[64,2048]{1,0:T(8,128)S(1)} %copy-done.4, s32[64,2048]{1,0:T(8,128)S(1)} %copy-done.5, bf16[256,256]{1,0:T(8,128)(2,1)S(1)} %copy-done.7), custom_call_target="tpu_custom_call" | custom-call | tf_op jit(solution)/shard_map/mirror/pallas_call | solution.py:529
  5.8 9.7 %all-to-all-start.1 = ((f32[32,16,128]{2,1,0:T(8,128)}), f32[32,16,128]{2,1,0:T(8,128)S(1)}, u32[]{:S(2)}, u32[]{:S(2)}) async-start(f32[32,16,128]{2,1,0:T(8,128)} %get-tuple-element.13), calls=%async_computation.1 | async-start | bytes 524288 | tf_op jit(solution)/shard_map/all_to_all | solution.py:549
  15.6 1.3 first.1
  16.9 0.0 copy-start.3
  16.9 0.0 copy-start.8
  16.9 0.0 copy-start.12
  16.9 0.0 copy-start.15
  16.9 0.0 copy-start.20
  16.9 7.5 %all-to-all-done.1.mirror = f32[32,16,128]{2,1,0:T(8,128)S(1)} async-done(((f32[32,16,128]{2,1,0:T(8,128)}), f32[32,16,128]{2,1,0:T(8,128)S(1)}, u32[]{:S(2)}, u32[]{:S(2)}) %all-to-all-start.1) | async-done | bytes 262176 | tf_op jit(solution)/shard_map/all_to_all | solution.py:549
  24.4 24.5 %all_to_all.35.got = f32[128,16,128]{2,1,0:T(8,128)S(1)} all-to-all(f32[128,16,128]{2,1,0:T(8,128)S(1)} %first.1), channel_id=1, replica_groups=mesh['mode'=4,'row'=32] {'mode','row'}, dimensions={0} | all-to-all | bytes 2097152 | tf_op jit(solution)/shard_map/all_to_all | solution.py:541
  49.0 3.1 %second.1 = (f32[128,16,128]{2,1,0:T(8,128)S(1)}, f32[16,64,256]{2,1,0:T(8,128)S(1)}, f32[16,16,256]{2,1,0:T(8,128)S(1)}) custom-call(f32[128,16,128]{2,1,0:T(8,128)S(1)} %all_to_all.35.got, f32[32,16,128]{2,1,0:T(8,128)S(1)} %all-to-all-done.1.mirror, f32[16,256]{1,0:T(8,128)S(1)} %copy-done.10, f32[16,256]{1,0:T(8,128)S(1)} %copy-done.6, ...), custom_call_target="tpu_custom_call" | custom-call | tf_op jit(solution)/shard_map/second/pallas_call | solution.py:529
  52.1 0.0 copy-start.11
  52.1 0.0 copy-start.18
  52.1 0.0 copy-start.19
  52.1 23.6 %all_to_all.36.got = f32[128,16,128]{2,1,0:T(8,128)S(1)} all-to-all(f32[128,16,128]{2,1,0:T(8,128)S(1)} %get-tuple-element.14), channel_id=1, replica_groups=mesh['mode'=4,'row'=32] {'mode','row'}, dimensions={0} | all-to-all | bytes 2097152 | tf_op jit(solution)/shard_map/all_to_all | solution.py:541
  75.7 3.3 %third.1 = (f32[128,16,128]{2,1,0:T(8,128)S(1)}, f32[128,16,128]{2,1,0:T(8,128)S(1)}) custom-call(f32[128,16,128]{2,1,0:T(8,128)S(1)} %all_to_all.36.got, f32[16,16,256]{2,1,0:T(8,128)S(1)} %get-tuple-element.15.mirror, f32[8,256]{1,0:T(8,128)S(1)} %copy-done.19, bf16[2,256,256]{2,1,0:T(8,128)(2,1)S(1)} %copy-done, f32[8,256]{1,0:T(8,128)S(1)} %copy-done.8, ...), custom_call_target="tpu_custom_call" | custom-call | tf_op jit(solution)/shard_map/third/pallas_call | solution.py:529
  79.1 23.6 %all_to_all.37.got = f32[128,16,128]{2,1,0:T(8,128)S(1)} all-to-all(f32[128,16,128]{2,1,0:T(8,128)S(1)} %get-tuple-element.16), channel_id=1, replica_groups=mesh['mode'=4,'row'=32] {'mode','row'}, dimensions={0} | all-to-all | bytes 2097152 | tf_op jit(solution)/shard_map/all_to_all | solution.py:541
  102.6 23.6 %all_to_all.38.got_cells = f32[128,16,128]{2,1,0:T(8,128)S(1)} all-to-all(f32[128,16,128]{2,1,0:T(8,128)S(1)} %get-tuple-element.17), channel_id=1, replica_groups=mesh['mode'=4,'row'=32] {'mode','row'}, dimensions={0} | all-to-all | bytes 2097152 | tf_op jit(solution)/shard_map/all_to_all | solution.py:541
  126.2 13.1 %fourth.1 = (f32[16,64,256]{2,1,0:T(8,128)S(1)}, f32[8,128]{1,0:T(8,128)S(1)}) custom-call(f32[128,16,128]{2,1,0:T(8,128)S(1)} %all_to_all.37.got, f32[128,16,128]{2,1,0:T(8,128)S(1)} %all_to_all.38.got_cells, f32[16,64,256]{2,1,0:T(8,128)S(1)} %get-tuple-element.18.cells, f32[16,16,256]{2,1,0:T(8,128)S(1)} %get-tuple-element.19.mirror, ...), custom_call_target="tpu_custom_call" | custom-call | tf_op jit(solution)/shard_map/fourth/pallas_call | solution.py:529
  139.4 0.0 copy-start.9
  139.4 0.0 copy-start.14
  139.4 18.0 %all_to_all.39.sums = f32[128,8,128]{2,1,0:T(8,128)S(1)} all-to-all(f32[128,8,128]{2,1,0:T(8,128)S(1)} %broadcast_in_dim.2), channel_id=1, replica_groups=mesh['mode'=4,'row'=32] {'mode','row'}, dimensions={0} | all-to-all | bytes 1048576 | tf_op jit(solution)/shard_map/all_to_all | solution.py:541
  157.4 4.1 %fifth.1 = (f32[128,16,128]{2,1,0:T(8,128)}, f32[64,128]{1,0:T(8,128)S(1)}) custom-call(f32[16,64,256]{2,1,0:T(8,128)S(1)} %get-tuple-element.20.cells, f32[128,8,128]{2,1,0:T(8,128)S(1)} %all_to_all.39.sums, f32[16,256]{1,0:T(8,128)S(1)} %copy-done.14, bf16[2,256,256]{2,1,0:T(8,128)(2,1)S(1)} %copy-done.3, f32[16,256]{1,0:T(8,128)S(1)} %copy-done.6, ...), custom_call_target="tpu_custom_call" | custom-call | tf_op jit(solution)/shard_map/fifth/pallas_call | solution.py:529
  161.5 4.8 %all-to-all-start.6 = ((f32[128,16,128]{2,1,0:T(8,128)}), f32[128,16,128]{2,1,0:T(8,128)S(1)}, u32[]{:S(2)}, u32[]{:S(2)}) async-start(f32[128,16,128]{2,1,0:T(8,128)} %get-tuple-element.22), calls=%async_computation.6 | async-start | bytes 2097152 | tf_op jit(solution)/shard_map/all_to_all | solution.py:541
  166.3 0.0 copy-start.13
  166.3 0.1 slice_reduce_fusion
  166.4 0.7 reshape_squeeze.3
  167.1 18.2 %all-to-all-done.6.got = f32[128,16,128]{2,1,0:T(8,128)S(1)} async-done(((f32[128,16,128]{2,1,0:T(8,128)}), f32[128,16,128]{2,1,0:T(8,128)S(1)}, u32[]{:S(2)}, u32[]{:S(2)}) %all-to-all-start.6) | async-done | bytes 1048608 | tf_op jit(solution)/shard_map/all_to_all | solution.py:541
  185.4 2.9 %last.1 = f32[1,2,64,2048]{3,2,1,0:T(8,128)} custom-call(f32[128,16,128]{2,1,0:T(8,128)S(1)} %all-to-all-done.6.got, f32[16,256]{1,0:T(8,128)S(1)} %copy-done.13, bf16[2,256,256]{2,1,0:T(8,128)(2,1)S(1)} %copy-done, f32[16,256]{1,0:T(8,128)S(1)} %copy-done.6, f32[16,256]{1,0:T(8,128)S(1)} %copy-done.9), custom_call_target="tpu_custom_call" | custom-call | tf_op jit(solution)/shard_map/last/pallas_call | solution.py:529
  (29 shorter events, 0.1 us)
Async XLA Ops:
  0.6 1.0 copy-start.4
  1.7 1.0 copy-start.5
  2.7 0.9 copy-start.7
  3.6 11.9 %copy-start.2 = (f32[1,2,64,2048]{3,2,1,0:T(8,128)S(1)}, f32[1,2,64,2048]{3,2,1,0:T(8,128)}, u32[]{:S(2)}) copy-start(f32[1,2,64,2048]{3,2,1,0:T(8,128)} %modes.1) | copy-start | bytes 3145732
  5.8 9.8 %copy-start = (bf16[2,256,256]{2,1,0:T(8,128)(2,1)S(1)}, bf16[2,256,256]{2,1,0:T(8,128)(2,1)}, u32[]{:S(2)}) copy-start(bf16[2,256,256]{2,1,0:T(8,128)(2,1)} %constant.40.clone.w) | copy-start | bytes 786436
  5.8 9.8 %copy-start.6 = (f32[16,256]{1,0:T(8,128)S(1)}, f32[16,256]{1,0:T(8,128)}, u32[]{:S(2)}) copy-start(f32[16,256]{1,0:T(8,128)} %constant.38.clone.twist) | copy-start | bytes 49156
  5.8 9.8 %copy-start.10 = (f32[16,256]{1,0:T(8,128)S(1)}, f32[16,256]{1,0:T(8,128)}, u32[]{:S(2)}) copy-start(f32[16,256]{1,0:T(8,128)} %constant.37.clone.nat) | copy-start | bytes 49156
  5.8 9.8 %copy-start.16 = (f32[16,256]{1,0:T(8,128)S(1)}, f32[16,256]{1,0:T(8,128)}, u32[]{:S(2)}) copy-start(f32[16,256]{1,0:T(8,128)} %constant.39.clone.post) | copy-start | bytes 49156
  5.8 18.7 %all-to-all-start.1 = ((f32[32,16,128]{2,1,0:T(8,128)}), f32[32,16,128]{2,1,0:T(8,128)S(1)}, u32[]{:S(2)}, u32[]{:S(2)}) async-start(f32[32,16,128]{2,1,0:T(8,128)} %get-tuple-element.13), calls=%async_computation.1 | async-start | bytes 524288 | tf_op jit(solution)/shard_map/all_to_all | solution.py:549
  16.9 32.1 %copy-start.1 = (bf16[2,256,256]{2,1,0:T(8,128)(2,1)S(1)}, bf16[2,256,256]{2,1,0:T(8,128)(2,1)}, u32[]{:S(2)}) copy-start(bf16[2,256,256]{2,1,0:T(8,128)(2,1)} %constant.42.clone.w_out) | copy-start | bytes 786436
  16.9 32.1 %copy-start.3 = (bf16[2,256,256]{2,1,0:T(8,128)(2,1)S(1)}, bf16[2,256,256]{2,1,0:T(8,128)(2,1)}, u32[]{:S(2)}) copy-start(bf16[2,256,256]{2,1,0:T(8,128)(2,1)} %constant.46.clone.w_in) | copy-start | bytes 786436
  16.9 32.1 %copy-start.8 = (f32[8,256]{1,0:T(8,128)S(1)}, f32[8,256]{1,0:T(8,128)}, u32[]{:S(2)}) copy-start(f32[8,256]{1,0:T(8,128)} %constant.44.clone.twist8) | copy-start | bytes 24580
  16.9 32.1 %copy-start.12 = (f32[8,256]{1,0:T(8,128)S(1)}, f32[8,256]{1,0:T(8,128)}, u32[]{:S(2)}) copy-start(f32[8,256]{1,0:T(8,128)} %constant.45.clone.post8) | copy-start | bytes 24580
  16.9 32.1 %copy-start.15 = (f32[16,256]{1,0:T(8,128)S(1)}, f32[16,256]{1,0:T(8,128)}, u32[]{:S(2)}) copy-start(f32[16,256]{1,0:T(8,128)} %constant.41.clone.post) | copy-start | bytes 49156
  16.9 32.1 %copy-start.20 = (f32[8,256]{1,0:T(8,128)S(1)}, f32[8,256]{1,0:T(8,128)}, u32[]{:S(2)}) copy-start(f32[8,256]{1,0:T(8,128)} %constant.43.clone.pre8) | copy-start | bytes 24580
  52.1 23.6 %copy-start.11 = (f32[8,256]{1,0:T(8,128)S(1)}, f32[8,256]{1,0:T(8,128)}, u32[]{:S(2)}) copy-start(f32[8,256]{1,0:T(8,128)} %constant.48.clone.nat8) | copy-start | bytes 24580
  52.1 23.6 %copy-start.18 = (f32[8,256]{1,0:T(8,128)S(1)}, f32[8,256]{1,0:T(8,128)}, u32[]{:S(2)}) copy-start(f32[8,256]{1,0:T(8,128)} %constant.49.clone.str8) | copy-start | bytes 24580
  52.1 23.6 %copy-start.19 = (f32[8,256]{1,0:T(8,128)S(1)}, f32[8,256]{1,0:T(8,128)}, u32[]{:S(2)}) copy-start(f32[8,256]{1,0:T(8,128)} %constant.47.clone.pre8) | copy-start | bytes 24580
  102.6 23.6 %copy-start.17 = (f32[8,256]{1,0:T(8,128)S(1)}, f32[8,256]{1,0:T(8,128)}, u32[]{:S(2)}) copy-start(f32[8,256]{1,0:T(8,128)} %constant.50.clone.post8) | copy-start | bytes 24580
  139.4 18.0 %copy-start.9 = (f32[16,256]{1,0:T(8,128)S(1)}, f32[16,256]{1,0:T(8,128)}, u32[]{:S(2)}) copy-start(f32[16,256]{1,0:T(8,128)} %constant.52.clone.post) | copy-start | bytes 49156
  139.4 18.0 %copy-start.14 = (f32[16,256]{1,0:T(8,128)S(1)}, f32[16,256]{1,0:T(8,128)}, u32[]{:S(2)}) copy-start(f32[16,256]{1,0:T(8,128)} %constant.51.clone.str_p) | copy-start | bytes 49156
  161.5 23.8 %all-to-all-start.6 = ((f32[128,16,128]{2,1,0:T(8,128)}), f32[128,16,128]{2,1,0:T(8,128)S(1)}, u32[]{:S(2)}, u32[]{:S(2)}) async-start(f32[128,16,128]{2,1,0:T(8,128)} %get-tuple-element.22), calls=%async_computation.6 | async-start | bytes 2097152 | tf_op jit(solution)/shard_map/all_to_all | solution.py:541
  166.3 19.1 %copy-start.13 = (f32[16,256]{1,0:T(8,128)S(1)}, f32[16,256]{1,0:T(8,128)}, u32[]{:S(2)}) copy-start(f32[16,256]{1,0:T(8,128)} %constant.53.clone.str16) | copy-start | bytes 49156

commit v2 on v1

--- a/solution.py
+++ b/solution.py
@@ -234,7 +234,7 @@
     for block in range(16):
         for b in range(2):
             out[2 * block + b] = tile[pl.ds(256 * b + block, 16, stride=16), :]
-    base = 32 * (x // 2) + lax.rem(x, 2)
+    base = 32 * lax.div(x, 2) + lax.rem(x, 2)
     for n in range(16):
         lanes = slice(LANES * n, LANES * n + LANES)
         lines[0, 64 * n : 64 * n + 64] = phase[:, lanes]
@@ -331,10 +331,18 @@
 
 
 def gram(left, right, same):
-    pairs = PAIRS if same else [(i, j) for i in range(4) for j in range(4)]
+    if same:
+        return gram_part(left, right, True, PAIRS)
+    rows = []
+    for i in (0, 2):
+        rows += gram_part(left, right, False, [(k, j) for k in (i, i + 1) for j in range(4)])
+    return rows
+
+
+def gram_part(left, right, same, pairs):
 
     def step(index, carry):
-        block, half = index // 2, lax.rem(index, 2)
+        block, half = lax.div(index, 2), lax.rem(index, 2)
         a, b = [], []
         for mode in range(4):
             rows = pl.ds(pl.multiple_of(16 * mode + 8 * half, 8), 8)
@@ -351,15 +359,12 @@
                 at += 1
         return tuple(result)
 
-    count = 16 if same else 32
-    zero = tuple(jnp.zeros((8, LANES), F32) for _ in range(count))
+    zero = tuple(jnp.zeros((8, LANES), F32) for _ in range(16))
     sums = lax.fori_loop(0, 32, step, zero)
     return [jnp.sum(value, axis=0, keepdims=True) for value in sums]
 
 
-def fourth_kernel(
-    got, got_cells, cells, mirror, nat8, twist8, w_out, post8, out, sums, src, tmp, middle
-):
+def fourth_kernel(got, mirror, nat8, twist8, w_out, post8, out, src, tmp):
     for parity in range(2):
         for block in range(8):
             sources = [row_source(parity, block, group) for group in range(8)]
@@ -367,7 +372,21 @@
             for mode in range(4):
                 rows = slice(16 * mode, 16 * mode + 16)
                 put(src, 8 * parity + block, rows, done[mode], done[4 + mode])
-            done = swap_bits([got_cells[at] for at in sources], (16, 32, 64))
+
+    def sink(block, re, im):
+        er, ei = split(mirror[block])
+        at = block // 2
+        er, ei = times(er, ei, *split(post8[at : at + 1]))
+        put(out, block, slice(None), *cell_times(re, im, er, ei))
+
+    to_strided(src, tmp, 8, nat8, twist8, w_out, sink)
+
+
+def middle_cells(got, tmp, out):
+    for parity in range(2):
+        for block in range(8):
+            sources = [row_source(parity, block, group) for group in range(8)]
+            done = swap_bits([got[at] for at in sources], (16, 32, 64))
             for mode in range(4):
                 rows = slice(16 * mode, 16 * mode + 16)
                 put(tmp, 8 * parity + block, rows, done[mode], done[4 + mode])
@@ -378,20 +397,7 @@
                 lanes = slice(LANES * plane, LANES * plane + LANES)
                 done = swap_bits([tmp[8 * parity + k, rows, lanes] for k in range(8)], (1, 2, 4))
                 for k in range(8):
-                    middle[2 * k + parity, rows, lanes] = done[k]
-
-    def sink(block, re, im):
-        er, ei = split(mirror[block])
-        at = block // 2
-        er, ei = times(er, ei, *split(post8[at : at + 1]))
-        put(out, block, slice(None), *cell_times(re, im, er, ei))
-
-    to_strided(src, tmp, 8, nat8, twist8, w_out, sink)
-    rows = gram(cells, cells, True) + gram(middle, middle, True) + gram(out, out, True)
-    rows += gram(cells, middle, False) + gram(middle, out, False)
-    rows.append(jnp.zeros((16, LANES), F32))
-    total = jnp.sum(jnp.concatenate(rows, axis=0).T, axis=0, keepdims=True)
-    sums[...] = jnp.broadcast_to(total, (8, LANES))
+                    out[2 * k + parity, rows, lanes] = done[k]
 
 
 def unpack_gram(values, start):
@@ -466,23 +472,8 @@
     return result
 
 
-def fifth_kernel(cells, sums, str_p, w_in, twist, post, out, ray, src, tmp):
-    total = jnp.sum(sums[...], axis=0)
-
-    def values(at):
-        return jnp.broadcast_to(total[:, at : at + 1], (8, LANES))
-
-    for step in range(2):
-        factor = inverse_factor(unpack_gram(values, 16 * step))
-        result = projected(factor, values, 48 + 32 * step)
-        for i in range(4):
-            for j in range(4):
-                for plane in range(2):
-                    at = 32 * step + 16 * plane + 4 * i + j
-                    ray[at : at + 1, :] = result[i, j][plane][0:1] * float(SIDE)
-    factor = inverse_factor(unpack_gram(values, 32))
+def mix(src, factor, out, tmp):
     factor = {key: (re * float(SIDE), im * float(SIDE)) for key, (re, im) in factor.items()}
-    to_natural(cells, tmp, src, 16, str_p, w_in, twist, post)
     for block in range(16):
         for half in range(2):
             base = 8 * half
@@ -521,68 +512,181 @@
 
 FIELD = (16, 64, 256)
 PACKETS = (128, 16, LANES)
-
-
-def run(kernel, name, args, tables, outs, scratch):
-    arrays = [jnp.asarray(TABLES[key]) for key in tables]
+KEYS = (
+    ("nat", 16), ("nat_gain", 16), ("str", 16), ("str_gain", 16), ("str_p", 16),
+    ("str_gain_p", 16), ("twist", 16), ("nat", 8), ("nat_gain", 8), ("str", 8),
+    ("str_gain", 8), ("str_p", 8), ("str_gain_p", 8), ("twist", 8), "w", "w_in", "w_out", "pick",
+)
+MESH = pl.DeviceIdType.MESH
+
+
+def shifted(index):
+    x, row = lax.axis_index("mode"), lax.axis_index("row")
+    z = lax.rem(lax.div(row, 8) + lax.div(lax.rem(index, 32), 8), 4)
+    y = lax.rem(lax.div(lax.rem(row, 8), 2) + lax.div(lax.rem(index, 8), 2), 4)
+    core = lax.rem(row + index, 2)
+    return lax.rem(x + lax.div(index, 32), 4), 8 * z + 2 * y + core
+
+
+def exchange_start(src, dst, send, recv, count):
+    x, row = lax.axis_index("mode"), lax.axis_index("row")
+    me = 32 * x + row if count == 128 else row
+
+    def step(index, carry):
+        to = shifted(index)
+        block = 32 * to[0] + to[1] if count == 128 else to[1]
+        pltpu.make_async_remote_copy(
+            src_ref=src.at[block], dst_ref=dst.at[me], send_sem=send, recv_sem=recv,
+            device_id=to, device_id_type=MESH,
+        ).start()
+        return carry
+
+    lax.fori_loop(1, count, step, 0)
+    dst[me] = src[me]
+
+    def whole():
+        return pltpu.make_async_remote_copy(
+            src_ref=src.at[pl.ds(0, count - 1)], dst_ref=dst.at[pl.ds(0, count - 1)],
+            send_sem=send, recv_sem=recv, device_id=shifted(1), device_id_type=MESH,
+        )
+
+    return whole()
+
+
+def group_start(src, dst, send, recv, near):
+    x, row = lax.axis_index("mode"), lax.axis_index("row")
+    zy, core = lax.div(row, 2), lax.rem(row, 2)
+    me = 2 * x + core if near else zy
+    count = 8 if near else 16
+
+    def partner(index):
+        if near:
+            to = shifted(32 * lax.div(index, 2) + lax.rem(index, 2))
+        else:
+            to = shifted(2 * index)
+        return to
+
+    def step(index, carry):
+        pltpu.make_async_remote_copy(
+            src_ref=src, dst_ref=dst.at[me], send_sem=send, recv_sem=recv,
+            device_id=partner(index), device_id_type=MESH,
+        ).start()
+        return carry
+
+    lax.fori_loop(1, count, step, 0)
+    dst[me] = src[...]
+    return pltpu.make_async_remote_copy(
+        src_ref=dst.at[pl.ds(0, count - 1)], dst_ref=dst.at[pl.ds(0, count - 1)],
+        send_sem=send, recv_sem=recv, device_id=partner(1), device_id_type=MESH,
+    )
+
+
+def totals(rows, part):
+    rows = rows + [jnp.zeros((LANES - len(rows), LANES), F32)]
+    total = jnp.sum(jnp.concatenate(rows, axis=0).T, axis=0, keepdims=True)
+    part[...] = jnp.broadcast_to(total, (8, LANES))
+
+
+def splat(total):
+    return lambda at: jnp.broadcast_to(total[:, at : at + 1], (8, LANES))
+
+
+def fused_kernel(*refs):
+    modes, phase, aperture = refs[:3]
+    t = dict(zip(KEYS, refs[3 : 3 + len(KEYS)]))
+    out, ray = refs[3 + len(KEYS) : 5 + len(KEYS)]
+    (
+        sent_e, got_e, sent_1, got_1, sent_2, got_2, sent_3, got_3, sent_m, got_m, sent_4, got_4,
+        rows_e, cols_e, cells_1, cells_2, cells_3, src, tmp, tile, lines,
+        part_a, near_a, part_b, far_b, part_c, near_c, part_d, far_d, send, recv,
+    ) = refs[5 + len(KEYS) :]
+    barrier = pltpu.get_barrier_semaphore()
+
+    def greet(index, carry):
+        pl.semaphore_signal(barrier, inc=1, device_id=shifted(index), device_id_type=MESH)
+        return carry
+
+    lax.fori_loop(1, 128, greet, 0)
+    first_kernel(
+        modes, t["nat", 16], t["twist", 16], t["str_gain", 16], t["w"], sent_1, src, tmp
+    )
+    pl.semaphore_wait(barrier, 127)
+    copy_1 = exchange_start(sent_1, got_1, send.at[0], recv.at[0], 128)
+    mirror_kernel(phase, aperture, t["pick"], sent_e, rows_e, tile, lines)
+    copy_e = exchange_start(sent_e, got_e, send.at[1], recv.at[1], 32)
+    copy_1.wait_recv()
+    copy_e.wait_recv()
+    second_kernel(
+        got_1, got_e, t["nat", 16], t["twist", 16], t["str_gain_p", 16], t["w_out"],
+        t["str_p", 8], t["twist", 8], t["nat_gain", 8], t["w_in"], sent_2, cells_1, cols_e, src, tmp,
+    )
+    copy_2 = exchange_start(sent_2, got_2, send.at[2], recv.at[2], 128)
+    copy_2.wait_recv()
+    third_kernel(
+        got_2, rows_e, t["str", 8], t["w"], t["twist", 8], t["nat_gain", 8], t["nat", 8],
+        t["str_gain", 8], sent_3, sent_m, src, tmp, tile.at[pl.ds(0, LANES)],
+    )
+    copy_3 = exchange_start(sent_3, got_3, send.at[3], recv.at[3], 128)
+    copy_m = exchange_start(sent_m, got_m, send.at[4], recv.at[4], 128)
+    copy_3.wait_recv()
+    fourth_kernel(got_3, cols_e, t["nat", 8], t["twist", 8], t["w_out"], t["str_gain_p", 8], cells_3, src, tmp)
+    totals(gram(cells_3, cells_3, True), part_a)
+    copy_a = group_start(part_a, near_a, send.at[5], recv.at[5], True)
+    to_natural(cells_3, tmp, src, 16, t["str_p", 16], t["w_in"], t["twist", 16], t["nat_gain", 16])
+    copy_a.wait_recv()
+    part_b[...] = jnp.sum(near_a[...], axis=0)
+    copy_b = group_start(part_b, far_b, send.at[6], recv.at[6], False)
+    copy_b.wait_recv()
+    factor = inverse_factor(unpack_gram(splat(jnp.sum(far_b[...], axis=0)), 0))
+    mix(src, factor, sent_4, tmp)
+    copy_4 = exchange_start(sent_4, got_4, send.at[7], recv.at[7], 128)
+    copy_m.wait_recv()
+    middle_cells(got_m, tmp, cells_2)
+    rows = gram(cells_1, cells_1, True) + gram(cells_2, cells_2, True)
+    rows += gram(cells_1, cells_2, False) + gram(cells_2, cells_3, False)
+    totals(rows, part_c)
+    copy_c = group_start(part_c, near_c, send.at[8], recv.at[8], True)
+    copy_c.wait_recv()
+    part_d[...] = jnp.sum(near_c[...], axis=0)
+    copy_d = group_start(part_d, far_d, send.at[9], recv.at[9], False)
+    copy_4.wait_recv()
+    last_kernel(got_4, t["str", 16], t["w"], t["twist", 16], t["nat_gain", 16], out, src, tmp)
+    copy_d.wait_recv()
+    values = splat(jnp.sum(far_d[...], axis=0))
+    for step in range(2):
+        factor = inverse_factor(unpack_gram(values, 16 * step))
+        result = projected(factor, values, 32 + 32 * step)
+        for i in range(4):
+            for j in range(4):
+                for plane in range(2):
+                    at = 32 * step + 16 * plane + 4 * i + j
+                    ray[at : at + 1, :] = result[i, j][plane][0:1] * float(SIDE)
+    for copy in (copy_1, copy_e, copy_2, copy_3, copy_m, copy_a, copy_b, copy_4, copy_c, copy_d):
+        copy.wait_send()
+
+
+def body(initial_modes, mirror_phase, aperture):
+    arrays = [jnp.asarray(TABLES[key]) for key in KEYS]
     whole = pl.BlockSpec(memory_space=pltpu.VMEM)
-    return pl.pallas_call(
-        kernel,
-        name=name,
-        in_specs=[whole] * (len(args) + len(arrays)),
-        out_specs=[whole] * len(outs),
-        out_shape=[jax.ShapeDtypeStruct(shape, F32) for shape in outs],
-        scratch_shapes=[pltpu.VMEM(shape, F32) for shape in scratch],
-        compiler_params=pltpu.CompilerParams(vmem_limit_bytes=48 * 1024 * 1024),
-    )(*args, *arrays)
-
-
-def exchange(packets):
-    return lax.all_to_all(packets, ("mode", "row"), split_axis=0, concat_axis=0, tiled=True)
-
-
-def body(initial_modes, mirror_phase, aperture):
-    mirror_send, mirror_rows = run(
-        mirror_kernel, "mirror", (mirror_phase, aperture), ["pick"],
-        [(32, 16, LANES), (16, 16, 256)], [(512, LANES), (2, 1024, LANES)],
-    )
-    mirror_got = lax.all_to_all(mirror_send, "row", split_axis=0, concat_axis=0, tiled=True)
-    (packets,) = run(
-        first_kernel, "first", (initial_modes,),
-        [("nat", 16), ("twist", 16), ("str_gain", 16), "w"], [PACKETS], [FIELD, FIELD],
-    )
-    got = exchange(packets)
-    packets, cells_one, mirror_columns_now = run(
-        second_kernel, "second", (got, mirror_got),
-        [("nat", 16), ("twist", 16), ("str_gain_p", 16), "w_out",
-         ("str_p", 8), ("twist", 8), ("nat_gain", 8), "w_in"],
-        [PACKETS, FIELD, (16, 16, 256)], [FIELD, FIELD],
-    )
-    got = exchange(packets)
-    packets, packets_cells = run(
-        third_kernel, "third", (got, mirror_rows),
-        [("str", 8), "w", ("twist", 8), ("nat_gain", 8), ("nat", 8), ("str_gain", 8)],
-        [PACKETS, PACKETS], [FIELD, FIELD, (LANES, LANES)],
-    )
-    got = exchange(packets)
-    got_cells = exchange(packets_cells)
-    cells_three, sums = run(
-        fourth_kernel, "fourth", (got, got_cells, cells_one, mirror_columns_now),
-        [("nat", 8), ("twist", 8), "w_out", ("str_gain_p", 8)],
-        [FIELD, (8, LANES)], [FIELD, FIELD, FIELD],
-    )
-    sums = exchange(jnp.broadcast_to(sums[None], (128, 8, LANES)))
-    packets, ray = run(
-        fifth_kernel, "fifth", (cells_three, sums),
-        [("str_p", 16), "w_in", ("twist", 16), ("nat_gain", 16)],
-        [PACKETS, (64, LANES)], [FIELD, FIELD],
-    )
-    got = exchange(packets)
-    (modes,) = run(
-        last_kernel, "last", (got,),
-        [("str", 16), "w", ("twist", 16), ("nat_gain", 16)],
-        [(1, 2, 64, SIDE)], [FIELD, FIELD],
-    )
+    small = (8, LANES)
+    shapes = [(32, 16, LANES)] * 2 + [PACKETS] * 10 + [(16, 16, 256)] * 2 + [FIELD] * 5
+    shapes += [(512, LANES), (2, 1024, LANES)]
+    shapes += [small, (8,) + small, small, (16,) + small] * 2
+    modes, ray = pl.pallas_call(
+        fused_kernel,
+        name="modes",
+        in_specs=[whole] * (3 + len(arrays)),
+        out_specs=[whole] * 2,
+        out_shape=[
+            jax.ShapeDtypeStruct((1, 2, 64, SIDE), F32),
+            jax.ShapeDtypeStruct((64, LANES), F32),
+        ],
+        scratch_shapes=[pltpu.VMEM(shape, F32) for shape in shapes]
+        + [pltpu.SemaphoreType.DMA((10,))] * 2,
+        compiler_params=pltpu.CompilerParams(
+            vmem_limit_bytes=56 * 1024 * 1024, collective_id=0, has_side_effects=True
+        ),
+    )(initial_modes, mirror_phase, aperture, *arrays)
     return modes, ray[:, 0].reshape(2, 2, 4, 4)
 
 

time: 189 us -> 120 us (0.63)
  blocking collectives: 113 us -> 0 us
  Pallas kernels: 30 us -> 115 us
  waiting for transfers between devices: 25.7 us -> 0 us
  starting transfers between devices: 14.5 us -> 0 us
    all_to_all x5 -> x0, blocking collectives: 113 us -> none  [exchange(): lax.all_to_all(packets, ('mode', 'row'), split_axis=0, concat_axis=0, til...]
    pallas_call x7 -> x1, Pallas kernels: 30 us -> 115 us  [body(): pl.pallas_call(fused_kernel, name='modes', in_specs=[whole] * (3 + len(ar...]
    all_to_all x2 -> x0, waiting for transfers between devices: 25.7 us -> none  [the longest x1 18.2 us: exchange(): lax.all_to_all(packets, ('mode', 'row'), split_axis=0, concat_axis=0, til...]
    all_to_all x2 -> x0, starting transfers between devices: 14.5 us -> none  [the longest x1 9.75 us: body(): lax.all_to_all(mirror_send, 'row', split_axis=0, concat_axis=0, tiled=True)]
  transfers between devices with their start and end apart: 2 -> 0, of which waited for: 2 -> 0; matrix products, arithmetic and copies ran while one was open for 0% -> 0% of each run, Pallas kernels for 1% -> 0%
where the time goes in v2:
time: 120 us
  Pallas kernels  115 us (96%)
  local copies, waits for them, and re-layouts  3.87 us (3%)
    pallas_call x1, Pallas kernels, body(): pl.pallas_call(fused_kernel, name='modes', in_specs=[whole] * (3 + len(ar...  115 us

profile of v2, /device:TPU:1, one launch (start us, length us, event | category | flops | bytes accessed | tf_op | source)
XLA Modules:
  0.0 119.5 jit_solution(7336204998600612552)
XLA Ops:
  0.6 115.0 %modes.1 = (f32[1,2,64,2048]{3,2,1,0:T(8,128)}, f32[64,128]{1,0:T(8,128)}) custom-call(f32[1,2,64,2048]{3,2,1,0:T(8,128)} %refs_0_.1, f32[64,2048]{1,0:T(8,128)} %refs_1_.1, s32[64,2048]{1,0:T(8,128)} %refs_2_.1, f32[16,256]{1,0:T(8,128)} %constant.36.clone.refs_3_, f32[16,256]{1,0:T(8,128)} %constant.37.clone.refs_4_, f32[16,256]{1,0:T(8,128)} %constant.38.clone.refs_5_, ...), custom_call_target="tpu_custom_call" | custom-call | tf_op jit(solution)/shard_map/modes/pallas_call | solution.py:675
  115.7 0.9 slice_reduce_fusion
  116.5 0.7 reshape_squeeze.3
  117.2 2.3 %copy.24 = f32[1,2,64,2048]{3,2,1,0:T(8,128)} copy(f32[1,2,64,2048]{3,2,1,0:T(8,128)} %get-tuple-element.8) | data formatting | bytes 2097152

commit v3 on v2

--- a/solution.py
+++ b/solution.py
@@ -102,7 +102,9 @@
     def dot(left, right):
         return jnp.dot(left, right, preferred_element_type=F32)
 
-    return dot(high, w_high) + dot(low, w_high) + dot(high, w_low)
+    count = values.shape[0]
+    both = dot(jnp.concatenate([high, low], axis=0), w_high)
+    return both[:count] + both[count:] + dot(high, w_low)
 
 
 def split(values):
@@ -129,14 +131,25 @@
     return arrays
 
 
+def swap_eight(arrays, stride):
+    lane = lax.broadcasted_iota(jnp.int32, arrays[0].shape, 1)
+    now = [pltpu.roll(a, stride * g, 1) if g else a for g, a in enumerate(arrays)]
+    for bit in (1, 2, 4):
+        on = (lane & (stride * bit)) != 0
+        now = [jnp.where(on, now[(g + bit) % 8], now[g]) for g in range(8)]
+    return [
+        pltpu.roll(now[-g % 8], LANES - stride * g, 1) if g else now[0] for g in range(8)
+    ]
+
+
 def put(ref, block, rows, re, im):
     ref[block, rows, :LANES] = re
     ref[block, rows, LANES:] = im
 
 
-def outer_dft(src, dst, outer, pre, post, index_in, index_out):
+def outer_dft(src, dst, outer, pre, post, index_in, index_out, base, size):
     def tile(step, carry):
-        rows = pl.ds(pl.multiple_of(step * 8, 8), 8)
+        rows = pl.ds(pl.multiple_of(base + step * 8, 8), 8)
         for group in range(16 // outer):
             values = []
             for n in range(outer):
@@ -153,7 +166,7 @@
                 put(dst, index_out(group, k), rows, re, im)
         return carry
 
-    lax.fori_loop(0, 8, tile, 0)
+    lax.fori_loop(0, size // 8, tile, 0)
 
 
 def natural_at(outer):
@@ -164,28 +177,31 @@
     return lambda group, n: (16 // outer) * n + group
 
 
-def to_strided(src, tmp, outer, pre, twist, w_ref, sink):
-    outer_dft(src, tmp, outer, pre, twist, natural_at(outer), strided_at(outer))
-    for part in range(4):
-        values = tmp[4 * part : 4 * part + 4].reshape(256, 256)
-        result = matmul(values, w_ref).reshape(4, 64, 256)
-        for n in range(4):
-            sink(4 * part + n, *split(result[n]))
-
-
-def to_natural(src, tmp, dst, outer, pre, w_ref, twist, post):
+def to_strided(src, tmp, outer, pre, twist, w_ref, sink, base=0, size=64):
+    outer_dft(src, tmp, outer, pre, twist, natural_at(outer), strided_at(outer), base, size)
+    step = 256 // size
+    for part in range(16 // step):
+        values = tmp[step * part : step * part + step, base : base + size].reshape(256, 256)
+        result = matmul(values, w_ref).reshape(step, size, 256)
+        for n in range(step):
+            sink(step * part + n, *split(result[n]))
+
+
+def to_natural(src, tmp, dst, outer, pre, w_ref, twist, post, base=0, size=64):
     groups = 16 // outer
-    for part in range(4):
+    step = 256 // size
+    rows = slice(base, base + size)
+    for part in range(16 // step):
         pieces = []
-        for n in range(4 * part, 4 * part + 4):
-            re, im = split(src[n])
-            if pre is not None:
-                at = n // groups
-                re, im = times(re, im, pre[at : at + 1, :LANES], pre[at : at + 1, LANES:])
+        for n in range(step * part, step * part + step):
+            re, im = split(src[n, rows])
+            at = n // groups
+            re, im = times(re, im, pre[at : at + 1, :LANES], pre[at : at + 1, LANES:])
             pieces.append(jnp.concatenate([re, im], axis=1))
         values = jnp.concatenate(pieces, axis=0)
-        tmp[4 * part : 4 * part + 4] = matmul(values, w_ref).reshape(4, 64, 256)
-    outer_dft(tmp, dst, outer, twist, post, strided_at(outer), natural_at(outer))
+        result = matmul(values, w_ref).reshape(step, size, 256)
+        tmp[step * part : step * part + step, rows] = result
+    outer_dft(tmp, dst, outer, twist, post, strided_at(outer), natural_at(outer), base, size)
 
 
 def turned(re, im):
@@ -264,76 +280,127 @@
             low, high = swap(got[4 * top + b], got[4 * top + 2 + b], 64)
             arrays[top, b, 0], arrays[top, b, 1] = low, high
     for plane in range(2):
-        done = swap_bits(
-            [arrays[index % 8, index // 8, plane] for index in range(16)], (1, 2, 4, 32)
-        )
+        done = []
+        for b in range(2):
+            done += swap_eight([arrays[index, b, plane] for index in range(8)], 1)
+        for index in range(8):
+            done[index], done[8 + index] = swap(done[index], done[8 + index], 32)
         for block in range(16):
             out[block, :, LANES * plane : LANES * plane + LANES] = done[block]
 
 
-def by_mode(values):
-    return values.reshape(4, 16, LANES)
-
-
 def cell_times(re, im, er, ei):
-    re, im = times(by_mode(re), by_mode(im), er[None], ei[None])
-    return re.reshape(64, LANES), im.reshape(64, LANES)
-
-
-def second_kernel(
-    got, mirror, nat, twist, post, w_out, pre8, twist8, post8, w_in, out, cells, mirror_out, src, tmp
-):
-    mirror_columns(mirror, mirror_out)
-    for mode in range(4):
+    shape = (re.shape[0] // 16, 16, LANES)
+    re, im = times(re.reshape(shape), im.reshape(shape), er[None], ei[None])
+    return re.reshape(-1, LANES), im.reshape(-1, LANES)
+
+
+def pack_pair(out, pieces, targets):
+    tile = jnp.concatenate(pieces, axis=0).T
+    for group in range(8):
+        at = 16 * group
+        done = swap(tile[at : at + 8], tile[at + 8 : at + 16], 64)
+        for b in range(2):
+            out[targets(b, group)] = done[b]
+
+
+def unpack_half(got, sources, src, block, half):
+    done = swap_eight([got[at] for at in sources], 16)
+    for mode in range(2):
+        for upper in range(2):
+            at = mode + 4 * upper
+            base = 16 * (2 * half + mode) + 8 * upper
+            put(src, block, slice(base, base + 8), done[at], done[at + 2])
+
+
+def second_lines(half, got, t, cells, src, tmp):
+    base = 32 * half
+    rows = slice(base, base + 32)
+    for mode in range(2 * half, 2 * half + 2):
         for n in range(16):
             re, im = swap(got[32 * mode + 2 * n], got[32 * mode + 2 * n + 1], 64)
             put(src, n, slice(16 * mode, 16 * mode + 16), re, im)
 
     def sink(block, re, im):
-        er, ei = split(mirror_out[block])
-        er, ei = times(er, ei, *split(post[block : block + 1]))
-        put(cells, block, slice(None), *cell_times(re, im, er, ei))
-
-    to_strided(src, tmp, 16, nat, twist, w_out, sink)
-    to_natural(cells, tmp, src, 8, pre8, w_in, twist8, post8)
+        put(cells, block, rows, re, im)
+
+    to_strided(src, tmp, 16, t["nat", 16], t["twist", 16], t["w_out"], sink, base, 32)
+
+
+def second_rest(half, mirror, t, out, cells, src, tmp):
+    base = 32 * half
+    rows = slice(base, base + 32)
+    for block in range(16):
+        er, ei = split(mirror[block])
+        er, ei = times(er, ei, *split(t["str_gain_p", 16][block : block + 1]))
+        put(cells, block, rows, *cell_times(*split(cells[block, rows]), er, ei))
+    to_natural(
+        cells, tmp, src, 8, t["str_p", 8], t["w_in"], t["twist", 8], t["nat_gain", 8], base, 32
+    )
+    for parity in range(2):
+        for pair in range(4):
+            pieces = []
+            for b in range(2):
+                pieces += split(src[8 * parity + 2 * pair + b, rows])
+            pack_pair(out, pieces, lambda b, group: row_source(parity, 2 * pair + b, group))
+
+
+def third_half(half, got, mirror, t, out, cells, src, tmp):
+    base = 32 * half
+    rows = slice(base, base + 32)
+    for block in range(16):
+        unpack_half(got, [column_source(block, group) for group in range(8)], src, block, half)
+    to_natural(
+        src, tmp, cells, 8, t["str", 8], t["w"], t["twist", 8], t["nat_gain", 8], base, 32
+    )
+    for block in range(16):
+        put(cells, block, rows, *cell_times(*split(cells[block, rows]), *split(mirror[block])))
+    held = []
+
+    def sink(block, re, im):
+        at = block // 2
+        held.extend(times(re, im, *split(t["str_gain", 8][at : at + 1])))
+        if block % 2:
+            pack_pair(out, list(held), lambda b, group: column_source(block - 1 + b, group))
+            held.clear()
+
+    to_strided(cells, tmp, 8, t["nat", 8], t["twist", 8], t["w"], sink, base, 32)
+
+
+def pack_cells(cells, out, tile):
+    for block in range(16):
+        tile[...] = turned(*split(cells[block]))
+        parity, k = block // 8, block % 8
+        for v in range(8):
+            out[column_source(2 * v + parity, k)] = tile[pl.ds(v, 16, stride=8), :]
+
+
+def fourth_half(half, got, mirror, t, cells, src, tmp):
+    base = 32 * half
+    rows = slice(base, base + 32)
     for parity in range(2):
         for block in range(8):
-            tile = turned(*split(src[8 * parity + block]))
-            for group in range(8):
-                out[row_source(parity, block, group)] = tile[16 * group : 16 * group + 16]
-
-
-def third_kernel(
-    got, mirror, pre8, w, twist8, post8, nat8, str8, out, out_cells, src, tmp, tile
-):
-    for block in range(16):
-        done = swap_bits([got[column_source(block, group)] for group in range(8)], (16, 32, 64))
-        for mode in range(4):
-            put(src, block, slice(16 * mode, 16 * mode + 16), done[mode], done[4 + mode])
-    to_natural(src, tmp, src, 8, pre8, w, twist8, post8)
-    for block in range(16):
-        re, im = cell_times(*split(src[block]), *split(mirror[block]))
-        put(src, block, slice(None), re, im)
-        tile[...] = turned(re, im)
-        parity, k = block // 8, block % 8
-        for v in range(8):
-            out_cells[column_source(2 * v + parity, k)] = tile[pl.ds(v, 16, stride=8), :]
+            sources = [row_source(parity, block, group) for group in range(8)]
+            unpack_half(got, sources, src, 8 * parity + block, half)
 
     def sink(block, re, im):
+        er, ei = split(mirror[block])
         at = block // 2
-        re, im = times(re, im, *split(str8[at : at + 1]))
-        send_columns(out, block, turned(re, im))
-
-    to_strided(src, tmp, 8, nat8, twist8, w, sink)
+        er, ei = times(er, ei, *split(t["str_gain_p", 8][at : at + 1]))
+        put(cells, block, rows, *cell_times(re, im, er, ei))
+
+    to_strided(src, tmp, 8, t["nat", 8], t["twist", 8], t["w_out"], sink, base, 32)
 
 
 PAIRS = [(i, j) for i in range(4) for j in range(i, 4)]
+EARLY = [(0, 0), (0, 1), (1, 1)]
+LATE = [pair for pair in PAIRS if pair not in EARLY]
 
 
 def gram(left, right, same):
+    rows = []
     if same:
-        return gram_part(left, right, True, PAIRS)
-    rows = []
+        return gram_part(left, right, True, EARLY) + gram_part(left, right, True, LATE)
     for i in (0, 2):
         rows += gram_part(left, right, False, [(k, j) for k in (i, i + 1) for j in range(4)])
     return rows
@@ -359,34 +426,17 @@
                 at += 1
         return tuple(result)
 
-    zero = tuple(jnp.zeros((8, LANES), F32) for _ in range(16))
+    count = sum(1 if same and i == j else 2 for i, j in pairs)
+    zero = tuple(jnp.zeros((8, LANES), F32) for _ in range(count))
     sums = lax.fori_loop(0, 32, step, zero)
     return [jnp.sum(value, axis=0, keepdims=True) for value in sums]
-
-
-def fourth_kernel(got, mirror, nat8, twist8, w_out, post8, out, src, tmp):
-    for parity in range(2):
-        for block in range(8):
-            sources = [row_source(parity, block, group) for group in range(8)]
-            done = swap_bits([got[at] for at in sources], (16, 32, 64))
-            for mode in range(4):
-                rows = slice(16 * mode, 16 * mode + 16)
-                put(src, 8 * parity + block, rows, done[mode], done[4 + mode])
-
-    def sink(block, re, im):
-        er, ei = split(mirror[block])
-        at = block // 2
-        er, ei = times(er, ei, *split(post8[at : at + 1]))
-        put(out, block, slice(None), *cell_times(re, im, er, ei))
-
-    to_strided(src, tmp, 8, nat8, twist8, w_out, sink)
 
 
 def middle_cells(got, tmp, out):
     for parity in range(2):
         for block in range(8):
             sources = [row_source(parity, block, group) for group in range(8)]
-            done = swap_bits([got[at] for at in sources], (16, 32, 64))
+            done = swap_eight([got[at] for at in sources], 16)
             for mode in range(4):
                 rows = slice(16 * mode, 16 * mode + 16)
                 put(tmp, 8 * parity + block, rows, done[mode], done[4 + mode])
@@ -395,7 +445,7 @@
             rows = slice(16 * mode, 16 * mode + 16)
             for plane in range(2):
                 lanes = slice(LANES * plane, LANES * plane + LANES)
-                done = swap_bits([tmp[8 * parity + k, rows, lanes] for k in range(8)], (1, 2, 4))
+                done = swap_eight([tmp[8 * parity + k, rows, lanes] for k in range(8)], 1)
                 for k in range(8):
                     out[2 * k + parity, rows, lanes] = done[k]
 
@@ -403,7 +453,7 @@
 def unpack_gram(values, start):
     table = {}
     at = start
-    for i, j in PAIRS:
+    for i, j in EARLY + LATE:
         if i == j:
             table[i, j] = (values(at), None)
             at += 1
@@ -501,7 +551,7 @@
 
 def last_kernel(got, str16, w, twist, post, out, src, tmp):
     for block in range(16):
-        done = swap_bits([got[column_source(block, group)] for group in range(8)], (16, 32, 64))
+        done = swap_eight([got[column_source(block, group)] for group in range(8)], 16)
         for q in range(4):
             put(src, block, slice(16 * q, 16 * q + 16), done[2 * q], done[2 * q + 1])
     to_natural(src, tmp, src, 16, str16, w, twist, post)
@@ -512,64 +562,93 @@
 
 FIELD = (16, 64, 256)
 PACKETS = (128, 16, LANES)
+HALVES = (2, 128, 8, LANES)
 KEYS = (
     ("nat", 16), ("nat_gain", 16), ("str", 16), ("str_gain", 16), ("str_p", 16),
     ("str_gain_p", 16), ("twist", 16), ("nat", 8), ("nat_gain", 8), ("str", 8),
-    ("str_gain", 8), ("str_p", 8), ("str_gain_p", 8), ("twist", 8), "w", "w_in", "w_out", "pick",
+    ("str_gain", 8), ("str_p", 8), ("str_gain_p", 8), ("twist", 8),
 )
+MATRICES = ("w", "w_in", "w_out")
+LINES = np.concatenate([TABLES[key] for key in KEYS])
+SQUARES = np.concatenate([TABLES[key] for key in MATRICES] + [TABLES["pick"][None]])
 MESH = pl.DeviceIdType.MESH
+
+
+def tables_in(lines, squares):
+    t = {}
+    start = 0
+    for key in KEYS:
+        t[key] = lines.at[pl.ds(start, key[1])]
+        start += key[1]
+    for index, key in enumerate(MATRICES):
+        t[key] = squares.at[pl.ds(2 * index, 2)]
+    t["pick"] = squares.at[2 * len(MATRICES)]
+    return t
 
 
 def shifted(index):
     x, row = lax.axis_index("mode"), lax.axis_index("row")
-    z = lax.rem(lax.div(row, 8) + lax.div(lax.rem(index, 32), 8), 4)
-    y = lax.rem(lax.div(lax.rem(row, 8), 2) + lax.div(lax.rem(index, 8), 2), 4)
-    core = lax.rem(row + index, 2)
-    return lax.rem(x + lax.div(index, 32), 4), 8 * z + 2 * y + core
-
-
-def exchange_start(src, dst, send, recv, count):
-    x, row = lax.axis_index("mode"), lax.axis_index("row")
-    me = 32 * x + row if count == 128 else row
+    by = lax.div(index, 4)
+    z = lax.rem(lax.div(row, 8) + lax.div(by, 8), 4)
+    y = lax.rem(lax.div(lax.rem(row, 8), 2) + lax.div(lax.rem(by, 8), 2), 4)
+    core = lax.rem(row + by, 2)
+    return lax.rem(x + lax.rem(index, 4), 4), 8 * z + 2 * y + core
+
+
+def exchange_part(src, dst, send, recv, start, stop):
+    me = 32 * lax.axis_index("mode") + lax.axis_index("row")
 
     def step(index, carry):
         to = shifted(index)
-        block = 32 * to[0] + to[1] if count == 128 else to[1]
         pltpu.make_async_remote_copy(
-            src_ref=src.at[block], dst_ref=dst.at[me], send_sem=send, recv_sem=recv,
+            src_ref=src.at[32 * to[0] + to[1]], dst_ref=dst.at[me], send_sem=send, recv_sem=recv,
             device_id=to, device_id_type=MESH,
         ).start()
         return carry
 
-    lax.fori_loop(1, count, step, 0)
+    lax.fori_loop(start, stop, step, 0)
+    if start > 1:
+        return None
     dst[me] = src[me]
-
-    def whole():
-        return pltpu.make_async_remote_copy(
-            src_ref=src.at[pl.ds(0, count - 1)], dst_ref=dst.at[pl.ds(0, count - 1)],
-            send_sem=send, recv_sem=recv, device_id=shifted(1), device_id_type=MESH,
-        )
-
-    return whole()
+    return pltpu.make_async_remote_copy(
+        src_ref=src.at[pl.ds(0, 127)], dst_ref=dst.at[pl.ds(0, 127)],
+        send_sem=send, recv_sem=recv, device_id=shifted(1), device_id_type=MESH,
+    )
+
+
+def exchange_start(src, dst, send, recv):
+    return exchange_part(src, dst, send, recv, 1, 128)
+
+
+def exchange_rows(src, dst, send, recv):
+    me = lax.axis_index("row")
+
+    def step(index, carry):
+        to = shifted(4 * index)
+        pltpu.make_async_remote_copy(
+            src_ref=src.at[to[1]], dst_ref=dst.at[me], send_sem=send, recv_sem=recv,
+            device_id=to, device_id_type=MESH,
+        ).start()
+        return carry
+
+    lax.fori_loop(1, 32, step, 0)
+    dst[me] = src[me]
+    return pltpu.make_async_remote_copy(
+        src_ref=src.at[pl.ds(0, 31)], dst_ref=dst.at[pl.ds(0, 31)],
+        send_sem=send, recv_sem=recv, device_id=shifted(4), device_id_type=MESH,
+    )
 
 
 def group_start(src, dst, send, recv, near):
     x, row = lax.axis_index("mode"), lax.axis_index("row")
-    zy, core = lax.div(row, 2), lax.rem(row, 2)
-    me = 2 * x + core if near else zy
+    me = x + 4 * lax.rem(row, 2) if near else lax.div(row, 2)
     count = 8 if near else 16
-
-    def partner(index):
-        if near:
-            to = shifted(32 * lax.div(index, 2) + lax.rem(index, 2))
-        else:
-            to = shifted(2 * index)
-        return to
+    stride = 1 if near else 8
 
     def step(index, carry):
         pltpu.make_async_remote_copy(
             src_ref=src, dst_ref=dst.at[me], send_sem=send, recv_sem=recv,
-            device_id=partner(index), device_id_type=MESH,
+            device_id=shifted(stride * index), device_id_type=MESH,
         ).start()
         return carry
 
@@ -577,7 +656,7 @@
     dst[me] = src[...]
     return pltpu.make_async_remote_copy(
         src_ref=dst.at[pl.ds(0, count - 1)], dst_ref=dst.at[pl.ds(0, count - 1)],
-        send_sem=send, recv_sem=recv, device_id=partner(1), device_id_type=MESH,
+        send_sem=send, recv_sem=recv, device_id=shifted(stride), device_id_type=MESH,
     )
 
 
@@ -591,15 +670,33 @@
     return lambda at: jnp.broadcast_to(total[:, at : at + 1], (8, LANES))
 
 
-def fused_kernel(*refs):
-    modes, phase, aperture = refs[:3]
-    t = dict(zip(KEYS, refs[3 : 3 + len(KEYS)]))
-    out, ray = refs[3 + len(KEYS) : 5 + len(KEYS)]
-    (
-        sent_e, got_e, sent_1, got_1, sent_2, got_2, sent_3, got_3, sent_m, got_m, sent_4, got_4,
-        rows_e, cols_e, cells_1, cells_2, cells_3, src, tmp, tile, lines,
-        part_a, near_a, part_b, far_b, part_c, near_c, part_d, far_d, send, recv,
-    ) = refs[5 + len(KEYS) :]
+def put_matrix(ray, step, table):
+    row = lax.broadcasted_iota(jnp.int32, (8, LANES), 0)
+    lane = lax.broadcasted_iota(jnp.int32, (8, LANES), 1)
+    for plane in range(2):
+        total = jnp.zeros((8, LANES), F32)
+        for (i, j), value in table.items():
+            total = jnp.where((row == i) & (lane == j), value[plane] * float(SIDE), total)
+        ray[step, plane] = total[:4, :4]
+
+
+def fused_kernel(
+    modes_in, phase_in, aperture_in, lines_in, squares_in, out, ray,
+    modes, phase, aperture, table_lines, table_squares,
+    sent_e, got_e, sent_1, got_1, sent_2, got_2, sent_3, got_3, sent_m, got_m, sent_4, got_4,
+    rows_e, cols_e, cells_1, cells_2, cells_3, src, tmp, tile, lines,
+    part_a, near_a, part_b, far_b, part_c, near_c, part_d, far_d, load, send, recv,
+):
+    loads = []
+    for index, (source, target) in enumerate(
+        (
+            (modes_in, modes), (lines_in, table_lines), (squares_in, table_squares),
+            (phase_in, phase), (aperture_in, aperture),
+        )
+    ):
+        loads.append(pltpu.make_async_copy(source, target, load.at[index]))
+        loads[-1].start()
+    t = tables_in(table_lines, table_squares)
     barrier = pltpu.get_barrier_semaphore()
 
     def greet(index, carry):
@@ -607,87 +704,104 @@
         return carry
 
     lax.fori_loop(1, 128, greet, 0)
+    for index in range(3):
+        loads[index].wait()
     first_kernel(
         modes, t["nat", 16], t["twist", 16], t["str_gain", 16], t["w"], sent_1, src, tmp
     )
     pl.semaphore_wait(barrier, 127)
-    copy_1 = exchange_start(sent_1, got_1, send.at[0], recv.at[0], 128)
+    copy_1 = exchange_start(sent_1, got_1, send.at[0], recv.at[0])
+    loads[3].wait()
+    loads[4].wait()
     mirror_kernel(phase, aperture, t["pick"], sent_e, rows_e, tile, lines)
-    copy_e = exchange_start(sent_e, got_e, send.at[1], recv.at[1], 32)
+    copy_e = exchange_rows(sent_e, got_e, send.at[1], recv.at[1])
     copy_1.wait_recv()
+    second_lines(0, got_1, t, cells_1, src, tmp)
+    second_lines(1, got_1, t, cells_1, src, tmp)
     copy_e.wait_recv()
-    second_kernel(
-        got_1, got_e, t["nat", 16], t["twist", 16], t["str_gain_p", 16], t["w_out"],
-        t["str_p", 8], t["twist", 8], t["nat_gain", 8], t["w_in"], sent_2, cells_1, cols_e, src, tmp,
+    mirror_columns(got_e, cols_e)
+    second_rest(0, cols_e, t, sent_2.at[0], cells_1, src, tmp)
+    copy_2a = exchange_start(sent_2.at[0], got_2.at[0], send.at[2], recv.at[2])
+    second_rest(1, cols_e, t, sent_2.at[1], cells_1, src, tmp)
+    copy_2b = exchange_start(sent_2.at[1], got_2.at[1], send.at[3], recv.at[3])
+    sums = gram(cells_1, cells_1, True)
+    copy_2a.wait_recv()
+    third_half(0, got_2.at[0], rows_e, t, sent_3.at[0], cells_2, src, tmp)
+    copy_3a = exchange_start(sent_3.at[0], got_3.at[0], send.at[4], recv.at[4])
+    copy_2b.wait_recv()
+    third_half(1, got_2.at[1], rows_e, t, sent_3.at[1], cells_2, src, tmp)
+    copy_3b = exchange_start(sent_3.at[1], got_3.at[1], send.at[5], recv.at[5])
+    pack_cells(cells_2, sent_m, tile.at[pl.ds(0, LANES)])
+    copy_m = exchange_part(sent_m, got_m, send.at[6], recv.at[6], 1, 33)
+    sums += gram(cells_2, cells_2, True)
+    copy_3a.wait_recv()
+    fourth_half(0, got_3.at[0], cols_e, t, cells_3, src, tmp)
+    sums += gram_part(cells_3, cells_3, True, EARLY)
+    copy_3b.wait_recv()
+    exchange_part(sent_m, got_m, send.at[6], recv.at[6], 33, 49)
+    fourth_half(1, got_3.at[1], cols_e, t, cells_3, src, tmp)
+    totals(sums + gram_part(cells_3, cells_3, True, LATE), part_a)
+    copy_a = group_start(part_a, near_a, send.at[7], recv.at[7], True)
+    exchange_part(sent_m, got_m, send.at[6], recv.at[6], 49, 69)
+    to_natural(
+        cells_3, tmp, src, 16, t["str_p", 16], t["w_in"], t["twist", 16], t["nat_gain", 16]
     )
-    copy_2 = exchange_start(sent_2, got_2, send.at[2], recv.at[2], 128)
-    copy_2.wait_recv()
-    third_kernel(
-        got_2, rows_e, t["str", 8], t["w"], t["twist", 8], t["nat_gain", 8], t["nat", 8],
-        t["str_gain", 8], sent_3, sent_m, src, tmp, tile.at[pl.ds(0, LANES)],
-    )
-    copy_3 = exchange_start(sent_3, got_3, send.at[3], recv.at[3], 128)
-    copy_m = exchange_start(sent_m, got_m, send.at[4], recv.at[4], 128)
-    copy_3.wait_recv()
-    fourth_kernel(got_3, cols_e, t["nat", 8], t["twist", 8], t["w_out"], t["str_gain_p", 8], cells_3, src, tmp)
-    totals(gram(cells_3, cells_3, True), part_a)
-    copy_a = group_start(part_a, near_a, send.at[5], recv.at[5], True)
-    to_natural(cells_3, tmp, src, 16, t["str_p", 16], t["w_in"], t["twist", 16], t["nat_gain", 16])
     copy_a.wait_recv()
     part_b[...] = jnp.sum(near_a[...], axis=0)
-    copy_b = group_start(part_b, far_b, send.at[6], recv.at[6], False)
+    copy_b = group_start(part_b, far_b, send.at[8], recv.at[8], False)
+    exchange_part(sent_m, got_m, send.at[6], recv.at[6], 69, 89)
     copy_b.wait_recv()
-    factor = inverse_factor(unpack_gram(splat(jnp.sum(far_b[...], axis=0)), 0))
+    values = splat(jnp.sum(far_b[...], axis=0))
+    factor = inverse_factor(unpack_gram(values, 32))
+    exchange_part(sent_m, got_m, send.at[6], recv.at[6], 89, 128)
     mix(src, factor, sent_4, tmp)
-    copy_4 = exchange_start(sent_4, got_4, send.at[7], recv.at[7], 128)
+    copy_4 = exchange_part(sent_4, got_4, send.at[9], recv.at[9], 1, 90)
     copy_m.wait_recv()
     middle_cells(got_m, tmp, cells_2)
-    rows = gram(cells_1, cells_1, True) + gram(cells_2, cells_2, True)
-    rows += gram(cells_1, cells_2, False) + gram(cells_2, cells_3, False)
-    totals(rows, part_c)
-    copy_c = group_start(part_c, near_c, send.at[8], recv.at[8], True)
+    totals(gram(cells_1, cells_2, False) + gram(cells_2, cells_3, False), part_c)
+    copy_c = group_start(part_c, near_c, send.at[10], recv.at[10], True)
+    exchange_part(sent_4, got_4, send.at[9], recv.at[9], 90, 128)
     copy_c.wait_recv()
     part_d[...] = jnp.sum(near_c[...], axis=0)
-    copy_d = group_start(part_d, far_d, send.at[9], recv.at[9], False)
+    copy_d = group_start(part_d, far_d, send.at[11], recv.at[11], False)
+    factors = [inverse_factor(unpack_gram(values, 16 * step)) for step in range(2)]
     copy_4.wait_recv()
     last_kernel(got_4, t["str", 16], t["w"], t["twist", 16], t["nat_gain", 16], out, src, tmp)
     copy_d.wait_recv()
     values = splat(jnp.sum(far_d[...], axis=0))
     for step in range(2):
-        factor = inverse_factor(unpack_gram(values, 16 * step))
-        result = projected(factor, values, 32 + 32 * step)
-        for i in range(4):
-            for j in range(4):
-                for plane in range(2):
-                    at = 32 * step + 16 * plane + 4 * i + j
-                    ray[at : at + 1, :] = result[i, j][plane][0:1] * float(SIDE)
-    for copy in (copy_1, copy_e, copy_2, copy_3, copy_m, copy_a, copy_b, copy_4, copy_c, copy_d):
+        put_matrix(ray, step, projected(factors[step], values, 32 * step))
+    for copy in (
+        copy_1, copy_e, copy_2a, copy_2b, copy_3a, copy_3b,
+        copy_m, copy_a, copy_b, copy_4, copy_c, copy_d,
+    ):
         copy.wait_send()
 
 
 def body(initial_modes, mirror_phase, aperture):
-    arrays = [jnp.asarray(TABLES[key]) for key in KEYS]
     whole = pl.BlockSpec(memory_space=pltpu.VMEM)
     small = (8, LANES)
-    shapes = [(32, 16, LANES)] * 2 + [PACKETS] * 10 + [(16, 16, 256)] * 2 + [FIELD] * 5
-    shapes += [(512, LANES), (2, 1024, LANES)]
-    shapes += [small, (8,) + small, small, (16,) + small] * 2
-    modes, ray = pl.pallas_call(
+    shapes = [((1, 2, 64, SIDE), F32), ((64, SIDE), F32), ((64, SIDE), jnp.int32)]
+    shapes += [(LINES.shape, F32), (SQUARES.shape, BF16)]
+    plain = [(32, 16, LANES)] * 2 + [PACKETS] * 2 + [HALVES] * 4 + [PACKETS] * 4
+    plain += [(16, 16, 256)] * 2 + [FIELD] * 5 + [(512, LANES), (2, 1024, LANES)]
+    plain += [small, (8,) + small, small, (16,) + small] * 2
+    shapes += [(shape, F32) for shape in plain]
+    return pl.pallas_call(
         fused_kernel,
         name="modes",
-        in_specs=[whole] * (3 + len(arrays)),
+        in_specs=[pl.BlockSpec(memory_space=pl.ANY)] * 5,
         out_specs=[whole] * 2,
         out_shape=[
             jax.ShapeDtypeStruct((1, 2, 64, SIDE), F32),
-            jax.ShapeDtypeStruct((64, LANES), F32),
+            jax.ShapeDtypeStruct((2, 2, 4, 4), F32),
         ],
-        scratch_shapes=[pltpu.VMEM(shape, F32) for shape in shapes]
-        + [pltpu.SemaphoreType.DMA((10,))] * 2,
+        scratch_shapes=[pltpu.VMEM(*shape) for shape in shapes]
+        + [pltpu.SemaphoreType.DMA((count,)) for count in (5, 12, 12)],
         compiler_params=pltpu.CompilerParams(
             vmem_limit_bytes=56 * 1024 * 1024, collective_id=0, has_side_effects=True
         ),
-    )(initial_modes, mirror_phase, aperture, *arrays)
-    return modes, ray[:, 0].reshape(2, 2, 4, 4)
+    )(initial_modes, mirror_phase, aperture, jnp.asarray(LINES), jnp.asarray(SQUARES))
 
 
 def solution(mesh):

time: 120 us -> 108 us (0.900)
  Pallas kernels: 115 us -> 104 us
    pallas_call x1, Pallas kernels: 115 us -> 104 us  [body(): pl.pallas_call(fused_kernel, name='modes', in_specs=[pl.BlockSpec(memory_...]
    unnamed x1 -> x4, local copies, waits for them, and re-layouts: 2.29 us -> 2.9 us
where the time goes in v3:
time: 108 us
  Pallas kernels  104 us (96%)
  local copies, waits for them, and re-layouts  2.9 us (3%)
    pallas_call x1, Pallas kernels, body(): pl.pallas_call(fused_kernel, name='modes', in_specs=[pl.BlockSpec(memory_...  104 us
    unnamed x4, local copies, waits for them, and re-layouts  2.9 us

profile of v3, /device:TPU:1, one launch (start us, length us, event | category | flops | bytes accessed | tf_op | source)
XLA Modules:
  0.0 107.5 jit_solution(14487459985637717775)
XLA Ops:
  0.6 104.0 %modes.1 = (f32[1,2,64,2048]{3,2,1,0:T(8,128)}, f32[2,2,4,4]{3,2,1,0:T(4,128)}) custom-call(f32[1,2,64,2048]{3,2,1,0:T(8,128)} %modes_in.1, f32[64,2048]{1,0:T(8,128)} %phase_in.1, s32[64,2048]{1,0:T(8,128)} %aperture_in.1, f32[168,256]{1,0:T(8,128)} %constant.4.clone.lines_in, bf16[7,256,256]{2,1,0:T(8,128)(2,1)} %constant.5.clone.squares_in), custom_call_target="tpu_custom_call" | custom-call | tf_op jit(solution)/shard_map/modes/pallas_call | solution.py:790
  104.6 0.0 copy-start
  104.6 2.3 %copy.9 = f32[1,2,64,2048]{3,2,1,0:T(8,128)} copy(f32[1,2,64,2048]{3,2,1,0:T(8,128)} %get-tuple-element.4) | data formatting | bytes 2097152
  106.9 0.0 copy-done
  106.9 0.6 copy.10
Async XLA Ops:
  104.6 2.3 %copy-start = (f32[2,2,4,4]{3,2,1,0:T(4,128)S(1)}, f32[2,2,4,4]{3,2,1,0:T(4,128)}, u32[]{:S(2)}) copy-start(f32[2,2,4,4]{3,2,1,0:T(4,128)} %get-tuple-element.5) | copy-start | bytes 772

commit v4 on v3

--- a/solution.py
+++ b/solution.py
@@ -595,48 +595,58 @@
     return lax.rem(x + lax.rem(index, 4), 4), 8 * z + 2 * y + core
 
 
-def exchange_part(src, dst, send, recv, start, stop):
-    me = 32 * lax.axis_index("mode") + lax.axis_index("row")
+CLASSES = sorted(
+    [(x, z, y) for x in range(3) for z in range(3) for y in range(3)],
+    key=lambda hops: (-sum(hops), hops),
+)
+
+
+def send_class(hops, src, dst, send, recv, rows_only):
+    x, row = lax.axis_index("mode"), lax.axis_index("row")
+    own = (x, lax.div(row, 8), lax.rem(lax.div(row, 2), 4))
+    core = lax.rem(row, 2)
+    me = row if rows_only else 32 * x + row
 
     def step(index, carry):
-        to = shifted(index)
+        rest = lax.div(index, 2)
+        to = []
+        for at, hop in zip(own, hops):
+            if hop == 1:
+                hop = 1 + 2 * lax.rem(rest, 2)
+                rest = lax.div(rest, 2)
+            to.append(lax.rem(at + hop, 4))
+        target = 8 * to[1] + 2 * to[2] + lax.rem(core + index + 1, 2)
+        block = target if rows_only else 32 * to[0] + target
         pltpu.make_async_remote_copy(
-            src_ref=src.at[32 * to[0] + to[1]], dst_ref=dst.at[me], send_sem=send, recv_sem=recv,
-            device_id=to, device_id_type=MESH,
+            src_ref=src.at[block], dst_ref=dst.at[me], send_sem=send, recv_sem=recv,
+            device_id=(to[0], target), device_id_type=MESH,
         ).start()
         return carry
 
-    lax.fori_loop(start, stop, step, 0)
-    if start > 1:
-        return None
+    count = 1 if sum(hops) == 0 else 2 ** (1 + hops.count(1))
+    lax.fori_loop(0, count, step, 0)
+
+
+def exchange_part(src, dst, send, recv, hops, rows_only=False):
+    for cls in CLASSES:
+        if sum(cls) in hops and not (rows_only and cls[0]):
+            send_class(cls, src, dst, send, recv, rows_only)
+
+
+def exchange_wait(src, dst, send, recv, rows_only=False):
+    row = lax.axis_index("row")
+    me = row if rows_only else 32 * lax.axis_index("mode") + row
     dst[me] = src[me]
+    count = 31 if rows_only else 127
     return pltpu.make_async_remote_copy(
-        src_ref=src.at[pl.ds(0, 127)], dst_ref=dst.at[pl.ds(0, 127)],
-        send_sem=send, recv_sem=recv, device_id=shifted(1), device_id_type=MESH,
-    )
-
-
-def exchange_start(src, dst, send, recv):
-    return exchange_part(src, dst, send, recv, 1, 128)
-
-
-def exchange_rows(src, dst, send, recv):
-    me = lax.axis_index("row")
-
-    def step(index, carry):
-        to = shifted(4 * index)
-        pltpu.make_async_remote_copy(
-            src_ref=src.at[to[1]], dst_ref=dst.at[me], send_sem=send, recv_sem=recv,
-            device_id=to, device_id_type=MESH,
-        ).start()
-        return carry
-
-    lax.fori_loop(1, 32, step, 0)
-    dst[me] = src[me]
-    return pltpu.make_async_remote_copy(
-        src_ref=src.at[pl.ds(0, 31)], dst_ref=dst.at[pl.ds(0, 31)],
+        src_ref=src.at[pl.ds(0, count)], dst_ref=dst.at[pl.ds(0, count)],
         send_sem=send, recv_sem=recv, device_id=shifted(4), device_id_type=MESH,
     )
+
+
+def exchange_start(src, dst, send, recv, rows_only=False):
+    exchange_part(src, dst, send, recv, range(7), rows_only)
+    return exchange_wait(src, dst, send, recv, rows_only)
 
 
 def group_start(src, dst, send, recv, near):
@@ -714,7 +724,7 @@
     loads[3].wait()
     loads[4].wait()
     mirror_kernel(phase, aperture, t["pick"], sent_e, rows_e, tile, lines)
-    copy_e = exchange_rows(sent_e, got_e, send.at[1], recv.at[1])
+    copy_e = exchange_start(sent_e, got_e, send.at[1], recv.at[1], True)
     copy_1.wait_recv()
     second_lines(0, got_1, t, cells_1, src, tmp)
     second_lines(1, got_1, t, cells_1, src, tmp)
@@ -732,35 +742,35 @@
     third_half(1, got_2.at[1], rows_e, t, sent_3.at[1], cells_2, src, tmp)
     copy_3b = exchange_start(sent_3.at[1], got_3.at[1], send.at[5], recv.at[5])
     pack_cells(cells_2, sent_m, tile.at[pl.ds(0, LANES)])
-    copy_m = exchange_part(sent_m, got_m, send.at[6], recv.at[6], 1, 33)
+    exchange_part(sent_m, got_m, send.at[6], recv.at[6], (6, 5, 4))
+    copy_m = exchange_wait(sent_m, got_m, send.at[6], recv.at[6])
     sums += gram(cells_2, cells_2, True)
     copy_3a.wait_recv()
     fourth_half(0, got_3.at[0], cols_e, t, cells_3, src, tmp)
     sums += gram_part(cells_3, cells_3, True, EARLY)
     copy_3b.wait_recv()
-    exchange_part(sent_m, got_m, send.at[6], recv.at[6], 33, 49)
     fourth_half(1, got_3.at[1], cols_e, t, cells_3, src, tmp)
     totals(sums + gram_part(cells_3, cells_3, True, LATE), part_a)
     copy_a = group_start(part_a, near_a, send.at[7], recv.at[7], True)
-    exchange_part(sent_m, got_m, send.at[6], recv.at[6], 49, 69)
+    exchange_part(sent_m, got_m, send.at[6], recv.at[6], (3,))
     to_natural(
         cells_3, tmp, src, 16, t["str_p", 16], t["w_in"], t["twist", 16], t["nat_gain", 16]
     )
     copy_a.wait_recv()
     part_b[...] = jnp.sum(near_a[...], axis=0)
     copy_b = group_start(part_b, far_b, send.at[8], recv.at[8], False)
-    exchange_part(sent_m, got_m, send.at[6], recv.at[6], 69, 89)
+    exchange_part(sent_m, got_m, send.at[6], recv.at[6], (2, 1, 0))
     copy_b.wait_recv()
     values = splat(jnp.sum(far_b[...], axis=0))
     factor = inverse_factor(unpack_gram(values, 32))
-    exchange_part(sent_m, got_m, send.at[6], recv.at[6], 89, 128)
     mix(src, factor, sent_4, tmp)
-    copy_4 = exchange_part(sent_4, got_4, send.at[9], recv.at[9], 1, 90)
+    exchange_part(sent_4, got_4, send.at[9], recv.at[9], (6, 5, 4, 3))
+    copy_4 = exchange_wait(sent_4, got_4, send.at[9], recv.at[9])
     copy_m.wait_recv()
     middle_cells(got_m, tmp, cells_2)
     totals(gram(cells_1, cells_2, False) + gram(cells_2, cells_3, False), part_c)
     copy_c = group_start(part_c, near_c, send.at[10], recv.at[10], True)
-    exchange_part(sent_4, got_4, send.at[9], recv.at[9], 90, 128)
+    exchange_part(sent_4, got_4, send.at[9], recv.at[9], (2, 1, 0))
     copy_c.wait_recv()
     part_d[...] = jnp.sum(near_c[...], axis=0)
     copy_d = group_start(part_d, far_d, send.at[11], recv.at[11], False)

time: 108 us -> 103 us (0.954)
  Pallas kernels: 104 us -> 99.2 us
    pallas_call x1, Pallas kernels: 104 us -> 99.2 us  [body(): pl.pallas_call(fused_kernel, name='modes', in_specs=[pl.BlockSpec(memory_...]
where the time goes in v4:
time: 103 us
  Pallas kernels  99.2 us (96%)
  local copies, waits for them, and re-layouts  2.9 us (3%)
    pallas_call x1, Pallas kernels, body(): pl.pallas_call(fused_kernel, name='modes', in_specs=[pl.BlockSpec(memory_...  99.2 us
    unnamed x4, local copies, waits for them, and re-layouts  2.9 us

profile of v4, /device:TPU:1, one launch (start us, length us, event | category | flops | bytes accessed | tf_op | source)
XLA Modules:
  0.0 102.7 jit_solution(690955140413809449)
XLA Ops:
  0.6 99.2 %modes.1 = (f32[1,2,64,2048]{3,2,1,0:T(8,128)}, f32[2,2,4,4]{3,2,1,0:T(4,128)}) custom-call(f32[1,2,64,2048]{3,2,1,0:T(8,128)} %modes_in.1, f32[64,2048]{1,0:T(8,128)} %phase_in.1, s32[64,2048]{1,0:T(8,128)} %aperture_in.1, f32[168,256]{1,0:T(8,128)} %constant.4.clone.lines_in, bf16[7,256,256]{2,1,0:T(8,128)(2,1)} %constant.5.clone.squares_in), custom_call_target="tpu_custom_call" | custom-call | tf_op jit(solution)/shard_map/modes/pallas_call | solution.py:800
  99.8 0.0 copy-start
  99.8 2.3 %copy.9 = f32[1,2,64,2048]{3,2,1,0:T(8,128)} copy(f32[1,2,64,2048]{3,2,1,0:T(8,128)} %get-tuple-element.4) | data formatting | bytes 2097152
  102.1 0.0 copy-done
  102.1 0.6 copy.10
Async XLA Ops:
  99.8 2.3 %copy-start = (f32[2,2,4,4]{3,2,1,0:T(4,128)S(1)}, f32[2,2,4,4]{3,2,1,0:T(4,128)}, u32[]{:S(2)}) copy-start(f32[2,2,4,4]{3,2,1,0:T(4,128)} %get-tuple-element.5) | copy-start | bytes 772

commit v5 on v4

--- a/solution.py
+++ b/solution.py
@@ -601,36 +601,35 @@
 )
 
 
-def send_class(hops, src, dst, send, recv, rows_only):
+def offsets_of(hops):
+    signs = [(1, 3) if hop == 1 else (hop,) for hop in hops]
+    return [
+        (x, z, y, core) for x in signs[0] for z in signs[1] for y in signs[2] for core in (1, 0)
+    ]
+
+
+def places(offsets):
     x, row = lax.axis_index("mode"), lax.axis_index("row")
-    own = (x, lax.div(row, 8), lax.rem(lax.div(row, 2), 4))
+    xs = [lax.rem(x + k, 4) for k in range(4)]
+    zs = [8 * lax.rem(lax.div(row, 8) + k, 4) for k in range(4)]
+    ys = [2 * lax.rem(lax.div(row, 2) + k, 4) for k in range(4)]
     core = lax.rem(row, 2)
-    me = row if rows_only else 32 * x + row
-
-    def step(index, carry):
-        rest = lax.div(index, 2)
-        to = []
-        for at, hop in zip(own, hops):
-            if hop == 1:
-                hop = 1 + 2 * lax.rem(rest, 2)
-                rest = lax.div(rest, 2)
-            to.append(lax.rem(at + hop, 4))
-        target = 8 * to[1] + 2 * to[2] + lax.rem(core + index + 1, 2)
-        block = target if rows_only else 32 * to[0] + target
+    cores = [core, 1 - core]
+    return [(xs[at[0]], zs[at[1]] + ys[at[2]] + cores[at[3]]) for at in offsets]
+
+
+def exchange_part(src, dst, send, recv, hops, rows_only=False):
+    row = lax.axis_index("row")
+    me = row if rows_only else 32 * lax.axis_index("mode") + row
+    offsets = [at for cls in CLASSES if sum(cls) in hops for at in offsets_of(cls) if any(at)]
+    if rows_only:
+        offsets = [at for at in offsets if not at[0]]
+    for to in places(offsets):
+        block = to[1] if rows_only else 32 * to[0] + to[1]
         pltpu.make_async_remote_copy(
             src_ref=src.at[block], dst_ref=dst.at[me], send_sem=send, recv_sem=recv,
-            device_id=(to[0], target), device_id_type=MESH,
+            device_id=to, device_id_type=MESH,
         ).start()
-        return carry
-
-    count = 1 if sum(hops) == 0 else 2 ** (1 + hops.count(1))
-    lax.fori_loop(0, count, step, 0)
-
-
-def exchange_part(src, dst, send, recv, hops, rows_only=False):
-    for cls in CLASSES:
-        if sum(cls) in hops and not (rows_only and cls[0]):
-            send_class(cls, src, dst, send, recv, rows_only)
 
 
 def exchange_wait(src, dst, send, recv, rows_only=False):
@@ -671,7 +670,7 @@
 
 
 def totals(rows, part):
-    rows = rows + [jnp.zeros((LANES - len(rows), LANES), F32)]
+    rows = rows + [jnp.zeros((LANES - sum(row.shape[0] for row in rows), LANES), F32)]
     total = jnp.sum(jnp.concatenate(rows, axis=0).T, axis=0, keepdims=True)
     part[...] = jnp.broadcast_to(total, (8, LANES))
 
@@ -709,11 +708,8 @@
     t = tables_in(table_lines, table_squares)
     barrier = pltpu.get_barrier_semaphore()
 
-    def greet(index, carry):
-        pl.semaphore_signal(barrier, inc=1, device_id=shifted(index), device_id_type=MESH)
-        return carry
-
-    lax.fori_loop(1, 128, greet, 0)
+    for to in places([at for hops in CLASSES for at in offsets_of(hops) if any(at)]):
+        pl.semaphore_signal(barrier, inc=1, device_id=to, device_id_type=MESH)
     for index in range(3):
         loads[index].wait()
     first_kernel(
@@ -734,7 +730,6 @@
     copy_2a = exchange_start(sent_2.at[0], got_2.at[0], send.at[2], recv.at[2])
     second_rest(1, cols_e, t, sent_2.at[1], cells_1, src, tmp)
     copy_2b = exchange_start(sent_2.at[1], got_2.at[1], send.at[3], recv.at[3])
-    sums = gram(cells_1, cells_1, True)
     copy_2a.wait_recv()
     third_half(0, got_2.at[0], rows_e, t, sent_3.at[0], cells_2, src, tmp)
     copy_3a = exchange_start(sent_3.at[0], got_3.at[0], send.at[4], recv.at[4])
@@ -744,10 +739,9 @@
     pack_cells(cells_2, sent_m, tile.at[pl.ds(0, LANES)])
     exchange_part(sent_m, got_m, send.at[6], recv.at[6], (6, 5, 4))
     copy_m = exchange_wait(sent_m, got_m, send.at[6], recv.at[6])
-    sums += gram(cells_2, cells_2, True)
     copy_3a.wait_recv()
     fourth_half(0, got_3.at[0], cols_e, t, cells_3, src, tmp)
-    sums += gram_part(cells_3, cells_3, True, EARLY)
+    sums = gram_part(cells_3, cells_3, True, EARLY)
     copy_3b.wait_recv()
     fourth_half(1, got_3.at[1], cols_e, t, cells_3, src, tmp)
     totals(sums + gram_part(cells_3, cells_3, True, LATE), part_a)
@@ -756,31 +750,35 @@
     to_natural(
         cells_3, tmp, src, 16, t["str_p", 16], t["w_in"], t["twist", 16], t["nat_gain", 16]
     )
+    later = gram(cells_2, cells_2, True)
     copy_a.wait_recv()
     part_b[...] = jnp.sum(near_a[...], axis=0)
     copy_b = group_start(part_b, far_b, send.at[8], recv.at[8], False)
     exchange_part(sent_m, got_m, send.at[6], recv.at[6], (2, 1, 0))
+    later = gram(cells_1, cells_1, True) + later
+    totals(later, part_c)
     copy_b.wait_recv()
-    values = splat(jnp.sum(far_b[...], axis=0))
-    factor = inverse_factor(unpack_gram(values, 32))
+    factor = inverse_factor(unpack_gram(splat(jnp.sum(far_b[...], axis=0)), 0))
     mix(src, factor, sent_4, tmp)
     exchange_part(sent_4, got_4, send.at[9], recv.at[9], (6, 5, 4, 3))
     copy_4 = exchange_wait(sent_4, got_4, send.at[9], recv.at[9])
     copy_m.wait_recv()
     middle_cells(got_m, tmp, cells_2)
-    totals(gram(cells_1, cells_2, False) + gram(cells_2, cells_3, False), part_c)
+    rows = [jnp.zeros((32, LANES), F32)] + gram(cells_1, cells_2, False)
+    totals(rows + gram(cells_2, cells_3, False), part_d)
+    part_c[...] += part_d[...]
     copy_c = group_start(part_c, near_c, send.at[10], recv.at[10], True)
     exchange_part(sent_4, got_4, send.at[9], recv.at[9], (2, 1, 0))
     copy_c.wait_recv()
     part_d[...] = jnp.sum(near_c[...], axis=0)
     copy_d = group_start(part_d, far_d, send.at[11], recv.at[11], False)
-    factors = [inverse_factor(unpack_gram(values, 16 * step)) for step in range(2)]
     copy_4.wait_recv()
     last_kernel(got_4, t["str", 16], t["w"], t["twist", 16], t["nat_gain", 16], out, src, tmp)
     copy_d.wait_recv()
     values = splat(jnp.sum(far_d[...], axis=0))
     for step in range(2):
-        put_matrix(ray, step, projected(factors[step], values, 32 * step))
+        factor = inverse_factor(unpack_gram(values, 16 * step))
+        put_matrix(ray, step, projected(factor, values, 32 + 32 * step))
     for copy in (
         copy_1, copy_e, copy_2a, copy_2b, copy_3a, copy_3b,
         copy_m, copy_a, copy_b, copy_4, copy_c, copy_d,

time: 103 us -> 94.5 us (0.917)
  Pallas kernels: 99.2 us -> 90.8 us
    pallas_call x1, Pallas kernels: 99.2 us -> 90.8 us  [body(): pl.pallas_call(fused_kernel, name='modes', in_specs=[pl.BlockSpec(memory_...]
where the time goes in v5:
time: 94.5 us; the launch traced here: 94.4 us
  Pallas kernels  90.8 us (96%)
  local copies, waits for them, and re-layouts  2.9 us (3%)
    pallas_call x1, Pallas kernels, body(): pl.pallas_call(fused_kernel, name='modes', in_specs=[pl.BlockSpec(memory_...  90.8 us
    unnamed x4, local copies, waits for them, and re-layouts  2.9 us

profile of v5, /device:TPU:1, one launch (start us, length us, event | category | flops | bytes accessed | tf_op | source)
XLA Modules:
  0.0 94.4 jit_solution(1545574644167287695)
XLA Ops:
  0.6 90.8 %modes.1 = (f32[1,2,64,2048]{3,2,1,0:T(8,128)}, f32[2,2,4,4]{3,2,1,0:T(4,128)}) custom-call(f32[1,2,64,2048]{3,2,1,0:T(8,128)} %modes_in.1, f32[64,2048]{1,0:T(8,128)} %phase_in.1, s32[64,2048]{1,0:T(8,128)} %aperture_in.1, f32[168,256]{1,0:T(8,128)} %constant.4.clone.lines_in, bf16[7,256,256]{2,1,0:T(8,128)(2,1)} %constant.5.clone.squares_in), custom_call_target="tpu_custom_call" | custom-call | tf_op jit(solution)/shard_map/modes/pallas_call | solution.py:798
  91.5 0.0 copy-start
  91.5 2.3 %copy.9 = f32[1,2,64,2048]{3,2,1,0:T(8,128)} copy(f32[1,2,64,2048]{3,2,1,0:T(8,128)} %get-tuple-element.4) | data formatting | bytes 2097152
  93.8 0.0 copy-done
  93.8 0.6 copy.10
Async XLA Ops:
  91.5 2.3 %copy-start = (f32[2,2,4,4]{3,2,1,0:T(4,128)S(1)}, f32[2,2,4,4]{3,2,1,0:T(4,128)}, u32[]{:S(2)}) copy-start(f32[2,2,4,4]{3,2,1,0:T(4,128)} %get-tuple-element.5) | copy-start | bytes 772

commit v6 on v5

--- a/solution.py
+++ b/solution.py
@@ -522,31 +522,51 @@
     return result
 
 
-def mix(src, factor, out, tmp):
-    factor = {key: (re * float(SIDE), im * float(SIDE)) for key, (re, im) in factor.items()}
+def swap_four(arrays, stride):
+    lane = lax.broadcasted_iota(jnp.int32, arrays[0].shape, 1)
+    now = [pltpu.roll(a, stride * g, 1) if g else a for g, a in enumerate(arrays)]
+    for bit in (1, 2):
+        on = (lane & (stride * bit)) != 0
+        now = [jnp.where(on, now[(g + bit) % 4], now[g]) for g in range(4)]
+    return [
+        pltpu.roll(now[-g % 4], LANES - stride * g, 1) if g else now[0] for g in range(4)
+    ]
+
+
+def ready(src, out, spun):
+    lane = lax.broadcasted_iota(jnp.int32, (16, LANES), 1)
+    real = (lane & 16) == 0
     for block in range(16):
-        for half in range(2):
-            base = 8 * half
-            fields = [
-                split(src[block, 16 * mode + base : 16 * mode + base + 8]) for mode in range(4)
-            ]
-            for j in range(4):
-                re = im = 0.0
-                for i in range(j + 1):
-                    pr, pi = times(*fields[i], *factor[i, j])
-                    re, im = re + pr, im + pi
-                rows = slice(16 * j + base, 16 * j + base + 8)
-                put(tmp, block, rows, re, im)
         pieces = []
         for mode in range(4):
-            rows = slice(16 * mode, 16 * mode + 16)
-            pieces += [tmp[block, rows, :LANES], tmp[block, rows, LANES:]]
+            pieces += split(src[block, 16 * mode : 16 * mode + 16])
         tile = jnp.concatenate(pieces, axis=0).T
         for half in range(2):
             parts = [tile[64 * half + 16 * q : 64 * half + 16 * q + 16] for q in range(4)]
-            done = swap_bits(parts, (32, 64))
-            for mode in range(4):
-                out[32 * mode + 2 * block + half] = done[mode]
+            for mode, value in enumerate(swap_four(parts, 32)):
+                at = 32 * mode + 2 * block + half
+                out[at] = value
+                spun[at] = jnp.where(
+                    real, -pltpu.roll(value, LANES - 16, 1), pltpu.roll(value, 16, 1)
+                )
+
+
+def mix(factor, out, spun):
+    factor = {key: (re * float(SIDE), im * float(SIDE)) for key, (re, im) in factor.items()}
+
+    def step(at, carry):
+        for rows in (slice(0, 8), slice(8, 16)):
+            plain = [out[32 * mode + at, rows] for mode in range(4)]
+            turn = [spun[32 * mode + at, rows] for mode in range(4)]
+            for j in range(4):
+                total = plain[j] * factor[j, j][0]
+                for i in range(j):
+                    re, im = factor[i, j]
+                    total = total + (plain[i] * re + turn[i] * im)
+                out[32 * j + at, rows] = total
+        return carry
+
+    lax.fori_loop(0, 32, step, 0)
 
 
 def last_kernel(got, str16, w, twist, post, out, src, tmp):
@@ -692,7 +712,7 @@
 def fused_kernel(
     modes_in, phase_in, aperture_in, lines_in, squares_in, out, ray,
     modes, phase, aperture, table_lines, table_squares,
-    sent_e, got_e, sent_1, got_1, sent_2, got_2, sent_3, got_3, sent_m, got_m, sent_4, got_4,
+    sent_e, got_e, sent_1, got_1, sent_2, got_2, sent_3, got_3, sent_m, got_m, sent_4, got_4, spun_4,
     rows_e, cols_e, cells_1, cells_2, cells_3, src, tmp, tile, lines,
     part_a, near_a, part_b, far_b, part_c, near_c, part_d, far_d, load, send, recv,
 ):
@@ -742,6 +762,7 @@
     copy_3a.wait_recv()
     fourth_half(0, got_3.at[0], cols_e, t, cells_3, src, tmp)
     sums = gram_part(cells_3, cells_3, True, EARLY)
+    totals(gram(cells_1, cells_1, True) + gram(cells_2, cells_2, True), part_c)
     copy_3b.wait_recv()
     fourth_half(1, got_3.at[1], cols_e, t, cells_3, src, tmp)
     totals(sums + gram_part(cells_3, cells_3, True, LATE), part_a)
@@ -750,16 +771,14 @@
     to_natural(
         cells_3, tmp, src, 16, t["str_p", 16], t["w_in"], t["twist", 16], t["nat_gain", 16]
     )
-    later = gram(cells_2, cells_2, True)
     copy_a.wait_recv()
     part_b[...] = jnp.sum(near_a[...], axis=0)
     copy_b = group_start(part_b, far_b, send.at[8], recv.at[8], False)
     exchange_part(sent_m, got_m, send.at[6], recv.at[6], (2, 1, 0))
-    later = gram(cells_1, cells_1, True) + later
-    totals(later, part_c)
+    ready(src, sent_4, spun_4)
     copy_b.wait_recv()
     factor = inverse_factor(unpack_gram(splat(jnp.sum(far_b[...], axis=0)), 0))
-    mix(src, factor, sent_4, tmp)
+    mix(factor, sent_4, spun_4)
     exchange_part(sent_4, got_4, send.at[9], recv.at[9], (6, 5, 4, 3))
     copy_4 = exchange_wait(sent_4, got_4, send.at[9], recv.at[9])
     copy_m.wait_recv()
@@ -791,7 +810,7 @@
     small = (8, LANES)
     shapes = [((1, 2, 64, SIDE), F32), ((64, SIDE), F32), ((64, SIDE), jnp.int32)]
     shapes += [(LINES.shape, F32), (SQUARES.shape, BF16)]
-    plain = [(32, 16, LANES)] * 2 + [PACKETS] * 2 + [HALVES] * 4 + [PACKETS] * 4
+    plain = [(32, 16, LANES)] * 2 + [PACKETS] * 2 + [HALVES] * 4 + [PACKETS] * 5
     plain += [(16, 16, 256)] * 2 + [FIELD] * 5 + [(512, LANES), (2, 1024, LANES)]
     plain += [small, (8,) + small, small, (16,) + small] * 2
     shapes += [(shape, F32) for shape in plain]

time: 94.5 us -> 93.6 us (level)
    pallas_call x1, Pallas kernels: 90.8 us -> 89.9 us  [body(): pl.pallas_call(fused_kernel, name='modes', in_specs=[pl.BlockSpec(memory_...]
where the time goes in v6:
time: 93.6 us; the launch traced here: 93.4 us
  Pallas kernels  89.9 us (96%)
  local copies, waits for them, and re-layouts  2.9 us (3%)
    pallas_call x1, Pallas kernels, body(): pl.pallas_call(fused_kernel, name='modes', in_specs=[pl.BlockSpec(memory_...  89.9 us
    unnamed x4, local copies, waits for them, and re-layouts  2.9 us

profile of v6, /device:TPU:1, one launch (start us, length us, event | category | flops | bytes accessed | tf_op | source)
XLA Modules:
  0.0 93.4 jit_solution(170842722538200464)
XLA Ops:
  0.6 89.9 %modes.1 = (f32[1,2,64,2048]{3,2,1,0:T(8,128)}, f32[2,2,4,4]{3,2,1,0:T(4,128)}) custom-call(f32[1,2,64,2048]{3,2,1,0:T(8,128)} %modes_in.1, f32[64,2048]{1,0:T(8,128)} %phase_in.1, s32[64,2048]{1,0:T(8,128)} %aperture_in.1, f32[168,256]{1,0:T(8,128)} %constant.4.clone.lines_in, bf16[7,256,256]{2,1,0:T(8,128)(2,1)} %constant.5.clone.squares_in), custom_call_target="tpu_custom_call" | custom-call | tf_op jit(solution)/shard_map/modes/pallas_call | solution.py:817
  90.5 0.0 copy-start
  90.5 2.3 %copy.9 = f32[1,2,64,2048]{3,2,1,0:T(8,128)} copy(f32[1,2,64,2048]{3,2,1,0:T(8,128)} %get-tuple-element.4) | data formatting | bytes 2097152
  92.8 0.0 copy-done
  92.8 0.6 copy.10
Async XLA Ops:
  90.5 2.3 %copy-start = (f32[2,2,4,4]{3,2,1,0:T(4,128)S(1)}, f32[2,2,4,4]{3,2,1,0:T(4,128)}, u32[]{:S(2)}) copy-start(f32[2,2,4,4]{3,2,1,0:T(4,128)} %get-tuple-element.5) | copy-start | bytes 772

commit v7 on v6

--- a/solution.py
+++ b/solution.py
@@ -762,7 +762,7 @@
     copy_3a.wait_recv()
     fourth_half(0, got_3.at[0], cols_e, t, cells_3, src, tmp)
     sums = gram_part(cells_3, cells_3, True, EARLY)
-    totals(gram(cells_1, cells_1, True) + gram(cells_2, cells_2, True), part_c)
+    sums = gram(cells_1, cells_1, True) + gram(cells_2, cells_2, True) + sums
     copy_3b.wait_recv()
     fourth_half(1, got_3.at[1], cols_e, t, cells_3, src, tmp)
     totals(sums + gram_part(cells_3, cells_3, True, LATE), part_a)
@@ -777,27 +777,26 @@
     exchange_part(sent_m, got_m, send.at[6], recv.at[6], (2, 1, 0))
     ready(src, sent_4, spun_4)
     copy_b.wait_recv()
-    factor = inverse_factor(unpack_gram(splat(jnp.sum(far_b[...], axis=0)), 0))
+    values = splat(jnp.sum(far_b[...], axis=0))
+    factor = inverse_factor(unpack_gram(values, 32))
     mix(factor, sent_4, spun_4)
     exchange_part(sent_4, got_4, send.at[9], recv.at[9], (6, 5, 4, 3))
     copy_4 = exchange_wait(sent_4, got_4, send.at[9], recv.at[9])
     copy_m.wait_recv()
     middle_cells(got_m, tmp, cells_2)
-    rows = [jnp.zeros((32, LANES), F32)] + gram(cells_1, cells_2, False)
-    totals(rows + gram(cells_2, cells_3, False), part_d)
-    part_c[...] += part_d[...]
+    totals(gram(cells_1, cells_2, False) + gram(cells_2, cells_3, False), part_c)
     copy_c = group_start(part_c, near_c, send.at[10], recv.at[10], True)
     exchange_part(sent_4, got_4, send.at[9], recv.at[9], (2, 1, 0))
     copy_c.wait_recv()
     part_d[...] = jnp.sum(near_c[...], axis=0)
     copy_d = group_start(part_d, far_d, send.at[11], recv.at[11], False)
+    factors = [inverse_factor(unpack_gram(values, 16 * step)) for step in range(2)]
     copy_4.wait_recv()
     last_kernel(got_4, t["str", 16], t["w"], t["twist", 16], t["nat_gain", 16], out, src, tmp)
     copy_d.wait_recv()
     values = splat(jnp.sum(far_d[...], axis=0))
     for step in range(2):
-        factor = inverse_factor(unpack_gram(values, 16 * step))
-        put_matrix(ray, step, projected(factor, values, 32 + 32 * step))
+        put_matrix(ray, step, projected(factors[step], values, 32 * step))
     for copy in (
         copy_1, copy_e, copy_2a, copy_2b, copy_3a, copy_3b,
         copy_m, copy_a, copy_b, copy_4, copy_c, copy_d,

time: 93.6 us -> 93.4 us (level)
  no operation moved by 1% of the time
where the time goes in v7:
time: 93.4 us; the launch traced here: 93.3 us
  Pallas kernels  89.7 us (96%)
  local copies, waits for them, and re-layouts  2.9 us (3%)
    pallas_call x1, Pallas kernels, body(): pl.pallas_call(fused_kernel, name='modes', in_specs=[pl.BlockSpec(memory_...  89.7 us
    unnamed x4, local copies, waits for them, and re-layouts  2.9 us

profile of v7, /device:TPU:1, one launch (start us, length us, event | category | flops | bytes accessed | tf_op | source)
XLA Modules:
  0.0 93.3 jit_solution(11275461184577606184)
XLA Ops:
  0.6 89.7 %modes.1 = (f32[1,2,64,2048]{3,2,1,0:T(8,128)}, f32[2,2,4,4]{3,2,1,0:T(4,128)}) custom-call(f32[1,2,64,2048]{3,2,1,0:T(8,128)} %modes_in.1, f32[64,2048]{1,0:T(8,128)} %phase_in.1, s32[64,2048]{1,0:T(8,128)} %aperture_in.1, f32[168,256]{1,0:T(8,128)} %constant.4.clone.lines_in, bf16[7,256,256]{2,1,0:T(8,128)(2,1)} %constant.5.clone.squares_in), custom_call_target="tpu_custom_call" | custom-call | tf_op jit(solution)/shard_map/modes/pallas_call | solution.py:816
  90.4 0.0 copy-start
  90.4 2.3 %copy.9 = f32[1,2,64,2048]{3,2,1,0:T(8,128)} copy(f32[1,2,64,2048]{3,2,1,0:T(8,128)} %get-tuple-element.4) | data formatting | bytes 2097152
  92.7 0.0 copy-done
  92.7 0.6 copy.10
Async XLA Ops:
  90.4 2.3 %copy-start = (f32[2,2,4,4]{3,2,1,0:T(4,128)S(1)}, f32[2,2,4,4]{3,2,1,0:T(4,128)}, u32[]{:S(2)}) copy-start(f32[2,2,4,4]{3,2,1,0:T(4,128)} %get-tuple-element.5) | copy-start | bytes 772
